TPU v7x, 128 devices: a whole 4x4x4 slice. The times are simulated.
128 devices in a mesh: sector: 2 (over core), slab: 64 (over z, y, x).
Axes of the slice: x: 4, y: 4, z: 4, core: 2. Of those that a mesh axis runs over, the one named last changes fastest.
Arguments:
- mode_basis: bfloat16 [64, 65536], replicated, may hold values from -6 to 6
- mode_coeff: bfloat16 [2048, 64], P(('sector', 'slab')), may hold values from -3 to 3
- reflect: bfloat16 [2048], P(('sector', 'slab')), may hold values from 0.29882812 to 1.5
- tile_row: int32 [2048], P(('sector', 'slab')), may hold values from 0 to 8191, as said below
- tile_col: int32 [2048], P(('sector', 'slab')), may hold values from 0 to 7936
- slot_live: int32 [2048], P(('sector', 'slab')), may hold values 0 or 1
Outputs:
- focal_plane: float32 [2, 8192, 8192], P(None, ('sector', 'slab'))
Inputs may be any that keep to these rules, and one draw needn't show every extreme that they name: Slot s belongs to the device at position s // 16 of the joined axes sector then slab; tile_row[s] // 128 equals (s // 16) % 64.
All inputs are finite; a program needn't handle non-finite values. No bound on the sum of `slot_live` on one device may be relied on, other than what follows from the above.
Results may differ from a plain program's by a relative error of at most 0.0007.
Values may be sent and summed in bfloat16 or wider, within the bound.
A program may use at most 192 MiB of HBM per device.

v0:
```python
import math

import jax
import jax.numpy as jnp
from jax import lax
from jax.sharding import PartitionSpec as P

GRID = 8192
TILE = 256


def passed_along(block, axis, distance):
    devices = range(lax.axis_size(axis))
    route = [(i - distance, i) for i in devices if i - distance in devices]
    return lax.ppermute(block, axis, route)


def hexagon(size):
    cells = jnp.arange(size, dtype=jnp.int32)
    across = jnp.abs(2 * cells - (size - 1))
    vertical = across[:, None]
    horizontal = across[None, :]
    radius = size - 2
    inside = (8 * vertical <= 7 * radius) & (7 * horizontal + 4 * vertical <= 7 * radius)
    return inside.astype(jnp.float32)


def render(
    mode_basis,
    mode_coeff,
    reflect,
    tile_row,
    tile_col,
    slot_live,
    base_row,
    height,
    width,
    tile_size,
):
    hex_mask = hexagon(tile_size)

    def deposit(slot_index, canvas):
        phases = jnp.dot(
            lax.dynamic_slice_in_dim(mode_coeff, slot_index, 1, 0),
            mode_basis,
            preferred_element_type=jnp.float32,
        ).reshape(tile_size, tile_size)
        weight = (
            reflect[slot_index].astype(jnp.float32)
            * slot_live[slot_index].astype(jnp.float32)
            * hex_mask
        )
        tile_piece = jnp.stack([weight * jnp.cos(phases), weight * jnp.sin(phases)])
        corner = (jnp.zeros((), jnp.int32), tile_row[slot_index] - base_row, tile_col[slot_index])
        current = lax.dynamic_slice(canvas, corner, (2, tile_size, tile_size))
        return lax.dynamic_update_slice(canvas, current + tile_piece, corner)

    canvas = jnp.zeros((2, height, width), jnp.float32)
    return lax.fori_loop(0, mode_coeff.shape[0], deposit, canvas)


def transform(real_part, imag_part, order_map, out_form):
    outer_len = real_part.shape[1]
    inner_len = real_part.shape[2]
    total_len = outer_len * inner_len
    highest = lax.Precision.HIGHEST
    outer_freq = jnp.arange(outer_len, dtype=jnp.int32)
    inner_freq = jnp.arange(inner_len, dtype=jnp.int32)
    first_turns = (order_map[:, None] * outer_freq[None, :] % outer_len).astype(jnp.float32) * (
        -2.0 * math.pi / outer_len
    )
    first_cos = jnp.cos(first_turns)
    first_sin = jnp.sin(first_turns)
    mid_real = jnp.einsum("bpi,pk->bki", real_part, first_cos, precision=highest) - jnp.einsum(
        "bpi,pk->bki", imag_part, first_sin, precision=highest
    )
    mid_imag = jnp.einsum("bpi,pk->bki", real_part, first_sin, precision=highest) + jnp.einsum(
        "bpi,pk->bki", imag_part, first_cos, precision=highest
    )
    twiddle = (outer_freq[:, None] * inner_freq[None, :] % total_len).astype(jnp.float32) * (
        -2.0 * math.pi / total_len
    )
    twist_cos = jnp.cos(twiddle)
    twist_sin = jnp.sin(twiddle)
    turned_real = mid_real * twist_cos - mid_imag * twist_sin
    turned_imag = mid_real * twist_sin + mid_imag * twist_cos
    second_turns = (inner_freq[:, None] * inner_freq[None, :] % inner_len).astype(jnp.float32) * (
        -2.0 * math.pi / inner_len
    )
    second_cos = jnp.cos(second_turns)
    second_sin = jnp.sin(second_turns)
    out_real = jnp.einsum(out_form, turned_real, second_cos, precision=highest) - jnp.einsum(
        out_form, turned_imag, second_sin, precision=highest
    )
    out_imag = jnp.einsum(out_form, turned_real, second_sin, precision=highest) + jnp.einsum(
        out_form, turned_imag, second_cos, precision=highest
    )
    return (out_real, out_imag)


def body(mode_basis, mode_coeff, reflect, tile_row, tile_col, slot_live):
    sectors = lax.axis_size("sector")
    slab_count = lax.axis_size("slab")
    devices = sectors * slab_count
    rows_dev = GRID // slab_count
    half_cols = GRID // sectors
    reach_slabs = (TILE + rows_dev - 2) // rows_dev
    slab_index = lax.axis_index("slab")
    params = (mode_coeff, reflect, tile_row, tile_col, slot_live)
    base_row = rows_dev * slab_index
    canvas = render(
        mode_basis,
        params[0],
        params[1],
        params[2],
        params[3],
        params[4],
        base_row,
        (reach_slabs + 1) * rows_dev,
        GRID,
        TILE,
    )
    band_count = reach_slabs + 1
    shaped = canvas.reshape(2, band_count * rows_dev, sectors, half_cols)
    out_shape = (2, band_count * rows_dev, half_cols)
    canvas = lax.psum_scatter(shaped, "sector", scatter_dimension=2, tiled=True).reshape(out_shape)
    field = canvas[:, :rows_dev]
    for hop_count in range(1, reach_slabs + 1):
        field = field + passed_along(
            canvas[:, hop_count * rows_dev : (hop_count + 1) * rows_dev], "slab", hop_count
        )
    field = lax.all_to_all(field, "sector", split_axis=1, concat_axis=2, tiled=True)
    line_count = GRID // devices
    natural = jnp.arange(devices, dtype=jnp.int32)
    row_real, row_imag = transform(
        field[0].reshape(line_count, devices, line_count),
        field[1].reshape(line_count, devices, line_count),
        natural,
        "bki,ij->jkb",
    )
    along_cols = jnp.stack([row_real.reshape(GRID, line_count), row_imag.reshape(GRID, line_count)])
    swapped = lax.all_to_all(
        along_cols, ("sector", "slab"), split_axis=1, concat_axis=2, tiled=True
    )
    order_map = natural % slab_count * sectors + natural // slab_count
    col_real, col_imag = transform(
        swapped[0].reshape(line_count, devices, line_count),
        swapped[1].reshape(line_count, devices, line_count),
        order_map,
        "bki,ij->bjk",
    )
    return (
        jnp.stack([col_real.reshape(line_count, GRID), col_imag.reshape(line_count, GRID)]) / GRID
    )


def solution(mesh):
    placed = (
        P(),
        P(("sector", "slab"), None),
        P(("sector", "slab")),
        P(("sector", "slab")),
        P(("sector", "slab")),
        P(("sector", "slab")),
    )
    return jax.shard_map(
        body,
        mesh=mesh,
        in_specs=placed,
        out_specs=P(None, ("sector", "slab"), None),
        check_vma=False,
    )
```

profile of v0, /device:TPU:1, one launch (start us, length us, event | category | flops | bytes accessed | tf_op | source)
XLA Modules:
  0.0 859.7 jit_solution(5738375730508495247)
XLA Ops:
  6.6 9.9 %broadcast_in_dim.2.clone = f32[2,384,8192]{1,2,0:T(8,128)} broadcast(f32[]{:T(128)} %constant.132.clone.1), dimensions={} | broadcast | bytes 25165828 | tf_op jit(solution)/shard_map/broadcast_in_dim | solution.py:58
  16.5 312.9 %while.14 = (s32[]{:T(128)}, f32[2,384,8192]{1,2,0:T(8,128)}, s32[16]{0:T(128)S(1)}, s32[]{:T(128)}, s32[16]{0:T(128)S(1)}, /*index=5*/bf16[16]{0:T(256)(128)(2,...) while((s32[]{:T(128)}, f32[2,384,8192]{1,2,0:T(8,128)}, ...), condition=%wide.region_1.0_spmd.clone, body=%wide.region_0.0_spmd.clone.sunk | while | flops 9043979 | bytes 15207987 | solution.py:59
  106.1 6.5 dynamic_update_slice.9
  125.8 6.5 dynamic_update_slice.9
  145.5 6.5 dynamic_update_slice.9
  165.2 6.5 dynamic_update_slice.9
  184.9 6.5 dynamic_update_slice.9
  224.3 6.5 dynamic_update_slice.9
  244.1 6.5 dynamic_update_slice.9
  283.5 6.6 dynamic_update_slice.9
  303.2 6.5 dynamic_update_slice.9
  330.7 89.6 %all-reduce.3.cloned.1.call-done = f32[2,384,2,4096]{1,3,2,0:T(8,128)} async-done(((f32[2,384,2,4096]{1,3,2,0:T(8,128)}), f32[2,384,2,4096]{1,3,2,0:T(8,128)}) %all-reduce.3.cloned.1.call-update) | async-done | bytes 25165840
  420.3 10.6 %dynamic-slice_bitcast_fusion = f32[2,384,4096]{1,2,0:T(8,128)} fusion(f32[2,384,2,4096]{1,3,2,0:T(8,128)} %all-reduce.3.cloned.1.call-done, u32[]{:T(128)} %bitcast.62), kind=kLoop, calls=%fused_computation.17 | loop fusion | bytes 25165828 | tf_op jit(solution)/shard_map/reshape | solution.py:126
  443.0 85.0 %collective-permute-done = f32[2,128,4096]{1,2,0:T(8,128)S(1)} collective-permute-done((f32[2,128,4096]{1,2,0:T(8,128)S(1)}, f32[2,128,4096]{1,2,0:T(8,128)S(1)}, u32[]{:S(2)}, u32[]{:S(2)}) %collective-permute-start) | collective-permute-done | bytes 4194336 | tf_op jit(solution)/shard_map/ppermute | solution.py:15
  528.0 89.9 %collective-permute-done.1 = f32[2,128,4096]{1,2,0:T(8,128)S(1)} collective-permute-done((f32[2,128,4096]{1,2,0:T(8,128)S(1)}, f32[2,128,4096]{1,2,0:T(8,128)S(1)}, u32[]{:S(2)}, u32[]{:S(2)}) %collective-permute-start.1) | collective-permute-done | bytes 4194336 | tf_op jit(solution)/shard_map/ppermute | solution.py:15
  622.8 7.3 copy.29
  630.1 9.3 %all_to_all.30 = f32[2,128,4096]{2,0,1:T(2,128)S(1)} all-to-all(f32[2,128,4096]{2,0,1:T(2,128)} %copy.29), channel_id=1, replica_groups=mesh['sector'=2,'slab'=64] {'sector'}, dimensions={1} | all-to-all | bytes 8388608 | tf_op jit(solution)/shard_map/all_to_all | solution.py:132
  694.8 11.8 %fusion.171 = f32[8192,2,64]{2,1,0:T(2,128)} fusion(f32[1,8192,64]{2,0,1:T(1,128)} %bitcast.170, f32[1,8192,64]{2,0,1:T(1,128)} %bitcast.169), kind=kLoop, calls=%fused_computation.184 | loop fusion | flops 1048576 | bytes 8388608
  706.6 11.1 %reshape.136 = f32[128,1,8192]{2,1,0:T(1,128)} reshape(f32[8192,2,64]{2,1,0:T(2,128)} %fusion.171) | data formatting | bytes 8388608
  717.7 10.7 %all-to-all-start.1 = ((f32[128,1,8192]{2,1,0:T(1,128)}), f32[128,1,8192]{2,1,0:T(1,128)}, u32[]{:S(2)}, u32[]{:S(2)}) async-start(f32[128,1,8192]{2,1,0:T(1,128)} %reshape.136), calls=%async_computation.1 | async-start | bytes 8388608 | tf_op jit(solution)/shard_map/all_to_all | solution.py:142
  728.5 52.2 %all-to-all-done.1 = f32[128,1,8192]{2,1,0:T(1,128)} async-done(((f32[128,1,8192]{2,1,0:T(1,128)}), f32[128,1,8192]{2,1,0:T(1,128)}, u32[]{:S(2)}, u32[]{:S(2)}) %all-to-all-start.1) | async-done | bytes 4194336 | tf_op jit(solution)/shard_map/all_to_all | solution.py:142
  781.3 13.9 %reduce = f32[128,8192]{1,0:T(8,128)} reduce(f32[128,1,8192]{2,1,0:T(1,128)} %all-to-all-done.1, f32[]{:T(128)} %broadcast.307), dimensions={1}, to_apply=%all_to_all.25.reduce_sub_computation | reduce | bytes 8388612 | tf_op jit(solution)/shard_map/all_to_all | solution.py:142
  795.1 9.6 %reshape.137 = f32[8192,2,64]{2,1,0:T(2,128)} reshape(f32[128,8192]{1,0:T(8,128)} %reduce) | data formatting | bytes 8388608
  804.7 11.3 %copy.40 = f32[2,128,64,64]{1,3,2,0:T(8,128)} copy(f32[2,128,64,64]{3,0,2,1:T(2,128)} %bitcast.158) | data formatting | bytes 8388608 | tf_op jit(solution)/shard_map/all_to_all | solution.py:142
  (229 shorter events, 309.9 us)
Async XLA Ops:
  6.5 413.8 %all-reduce.3.cloned.1.call-start = ((), (), s32[]{:S(2)}) async-start(), calls=%async_computation.2 | async-start | bytes 50331648
  6.6 10.0 %copy-start.4 = (s32[16]{0:T(128)S(1)}, s32[16]{0:T(128)}, u32[]{:S(2)}) copy-start(s32[16]{0:T(128)} %param.11) | copy-start | bytes 196
  6.6 10.0 %copy-start.5 = (s32[16]{0:T(128)S(1)}, s32[16]{0:T(128)}, u32[]{:S(2)}) copy-start(s32[16]{0:T(128)} %param.12) | copy-start | bytes 196
  6.6 10.0 %copy-start.6 = (bf16[16]{0:T(256)(128)(2,1)S(1)}, bf16[16]{0:T(256)(128)(2,1)}, u32[]{:S(2)}) copy-start(bf16[16]{0:T(256)(128)(2,1)} %param.10) | copy-start | bytes 100
  6.6 9.9 %copy-start.7 = (s32[16]{0:T(128)S(1)}, s32[16]{0:T(128)}, u32[]{:S(2)}) copy-start(s32[16]{0:T(128)} %param.13) | copy-start | bytes 196
  329.5 0.7 copy-start.8
  435.0 93.0 %collective-permute-start = (f32[2,128,4096]{1,2,0:T(8,128)S(1)}, f32[2,128,4096]{1,2,0:T(8,128)S(1)}, u32[]{:S(2)}, u32[]{:S(2)}) collective-permute-start(f32[2,128,4096]{1,2,0:T(8,128)S(1)} %get-tuple-element.230), channel_id=1, source_target_pairs={{0,1},{1,2},{2,3},{3,4},{4,5},{5,6},{6,7},{7,8},{8,9},{9,10},{10,1... | collective-permute-start | bytes 12582920 | tf_op jit(solution)/shard_map/ppermute | solution.py:15
  438.5 179.4 %collective-permute-start.1 = (f32[2,128,4096]{1,2,0:T(8,128)S(1)}, f32[2,128,4096]{1,2,0:T(8,128)S(1)}, u32[]{:S(2)}, u32[]{:S(2)}) collective-permute-start(f32[2,128,4096]{1,2,0:T(8,128)S(1)} %get-tuple-element.231), channel_id=1, source_target_pairs={{0,2},{1,3},{2,4},{3,5},{4,6},{5,7},{6,8},{7,9},{8,10},{9,11},{10,... | collective-permute-start | bytes 12582920 | tf_op jit(solution)/shard_map/ppermute | solution.py:15
  655.4 3.4 copy-start.2
  669.5 2.1 copy-start
  669.5 2.2 copy-start.1
  717.7 63.0 %all-to-all-start.1 = ((f32[128,1,8192]{2,1,0:T(1,128)}), f32[128,1,8192]{2,1,0:T(1,128)}, u32[]{:S(2)}, u32[]{:S(2)}) async-start(f32[128,1,8192]{2,1,0:T(1,128)} %reshape.136), calls=%async_computation.1 | async-start | bytes 8388608 | tf_op jit(solution)/shard_map/all_to_all | solution.py:142
  845.6 2.9 copy-start.3
Sparse Core Ops, SparseCore 0:
  329.6 90.6 all-reduce.2
where the time goes:
time: 874 us; the launch traced here: 860 us
  waiting for transfers between devices  317 us (36%)
  local copies, waits for them, and re-layouts  271 us (31%)
  matrix products  122 us (14%)
  loops' own time  54.7 us (6%)
  other arithmetic  54 us (6%)
  starting transfers between devices  18.5 us (2%)
  between operations  14.1 us (2%)
  blocking collectives  9.32 us (1%)
    ppermute x2, waiting for transfers between devices, passed_along(): return lax.ppermute(block, axis, route)  175 us
    dynamic_update_slice x32, local copies, waits for them, and re-layouts, deposit(): return lax.dynamic_update_slice(canvas, current + tile_piece, corner)  105 us
    unnamed x2, waiting for transfers between devices  89.6 us
    dot_general x16, matrix products, deposit(): jnp.dot(lax.dynamic_slice_in_dim(mode_coeff, slot_index, 1, 0), mode_basi...  73.6 us
    another operation x1, loops' own time, render(): return lax.fori_loop(0, mode_coeff.shape[0], deposit, canvas)  54.7 us
    all_to_all x1, waiting for transfers between devices, body(): lax.all_to_all(along_cols, ('sector', 'slab'), split_axis=1, concat_axis=...  52.2 us
    dynamic_slice x32, local copies, waits for them, and re-layouts, deposit(): current = lax.dynamic_slice(canvas, corner, (2, tile_size, tile_size))  24.9 us
    unnamed x21, local copies, waits for them, and re-layouts  22 us
  transfers between devices with their start and end apart: 4, of which 4 were waited for; matrix products, arithmetic and copies ran while one was open for 0% of the time, Pallas kernels for 0%

commit v1 on v0

v1 whole, which is shorter than its diff:
```python
import functools
import math

import jax
import jax.numpy as jnp
import ml_dtypes
import numpy as np
from jax import lax
from jax.experimental import pallas as pl
from jax.experimental.pallas import tpu as pltpu
from jax.sharding import PartitionSpec as P

GRID = 8192
TILE = 256
SLOTS = 16
MODES = 64
SLABS = 64
DEVICES = 128
LINES = GRID // DEVICES
BLOCKS = GRID // 128
NEAR = 6 * SLOTS
CHUNK = 16
CHUNKS = LINES // CHUNK
PAD = 16
HALF = 32
MESH = pl.DeviceIdType.MESH
F32 = jnp.float32
BF16 = jnp.bfloat16

LOW = 12.0
STEPS = 32766.0 / (LOW + 15.25)


def polynomial(values, powers):
    spots = np.cos(np.pi * (np.arange(400) + 0.5) / 800) * 0.5
    table = np.stack([spots**power for power in powers], axis=1)
    return [float(c) for c in np.linalg.lstsq(table, values(np.pi * spots), rcond=None)[0]]


SIN_TERMS = polynomial(np.sin, (1, 3, 5, 7, 9))
COS_TERMS = polynomial(np.cos, (0, 2, 4, 6, 8))


def halves(table):
    high = table.astype(ml_dtypes.bfloat16)
    low = (table - high.astype(np.float64)).astype(ml_dtypes.bfloat16)
    return high, low


def angles(left, right, total):
    turns = np.outer(np.arange(left), np.arange(right)) % total
    return 2.0 * math.pi * turns / total


def tables():
    first = angles(64, 64, 64)
    col_first = np.block([[np.cos(first), np.sin(first)], [-np.sin(first), np.cos(first)]])
    high, low = halves(col_first)
    col_first_both = np.concatenate([high, high], axis=1)
    twist = angles(64, 128, GRID)
    col_twist = np.stack([np.cos(twist), np.sin(twist)]).astype(np.float32)
    second = angles(128, 128, 128)
    col_second = np.concatenate(halves(np.concatenate([np.cos(second), np.sin(second)], axis=1)))
    row_first = np.stack(
        halves(np.block([[np.cos(second), -np.sin(second)], [np.sin(second), np.cos(second)]]))
    )
    last_high, last_low = halves(col_first / GRID)
    last_both = np.concatenate([last_high, last_high], axis=1)
    return (
        (col_first_both, low, col_twist, col_second, row_first, col_twist),
        (last_both, last_low),
    )


def split(value):
    high = value.astype(BF16)
    return high, (value - high.astype(F32)).astype(BF16)


def dot(left, right):
    return jnp.dot(left, right, preferred_element_type=F32)


def dot_lanes(left, right):
    return lax.dot_general(left, right, (((1,), (1,)), ((), ())), preferred_element_type=F32)


def gather_kernel(own_ref, near_ref, send_sem, recv_sem):
    sector = lax.axis_index("sector")
    slab = lax.axis_index("slab")
    barrier = pltpu.get_barrier_semaphore()
    others = [(flip, hop) for hop in range(3) for flip in range(2)][1:]
    for flip, hop in others:
        for step in {hop, -hop}:
            pl.semaphore_signal(
                barrier,
                inc=1,
                device_id=(lax.rem(sector + flip, 2), lax.rem(slab + step + SLABS, SLABS)),
                device_id_type=MESH,
            )
    near_ref[0, sector] = own_ref[...]
    pl.semaphore_wait(barrier, 9)
    copies = []
    for number, (flip, hop) in enumerate(others):
        copy = pltpu.make_async_remote_copy(
            src_ref=own_ref,
            dst_ref=near_ref.at[hop, sector],
            send_sem=send_sem.at[number],
            recv_sem=recv_sem.at[number],
            device_id=(lax.rem(sector + flip, 2), lax.rem(slab + hop, SLABS)),
            device_id_type=MESH,
        )
        copy.start()
        copies.append(copy)
    for copy in copies:
        copy.wait()


def gather_near(own):
    return pl.pallas_call(
        gather_kernel,
        out_shape=jax.ShapeDtypeStruct((3, 2, SLOTS, 128), F32),
        in_specs=[pl.BlockSpec(memory_space=pltpu.VMEM)],
        out_specs=pl.BlockSpec(memory_space=pltpu.VMEM),
        scratch_shapes=[pltpu.SemaphoreType.DMA((5,)), pltpu.SemaphoreType.DMA((5,))],
        compiler_params=pltpu.CompilerParams(collective_id=0, has_side_effects=True),
        name="gather_near",
    )(own)


def circle(phase):
    turns = phase * (0.5 / math.pi)
    part = turns - jnp.round(turns)
    square = part * part
    sine = SIN_TERMS[-1]
    for term in SIN_TERMS[-2::-1]:
        sine = sine * square + term
    sine = sine * part
    cosine = COS_TERMS[-1]
    for term in COS_TERMS[-2::-1]:
        cosine = cosine * square + term
    double = sine + sine
    return 1.0 - double * sine, double * cosine


BASIS_PARTS = 8


def render_kernel(
    slot_ref, coeff_ref, basis_hbm, field_hbm, basis, left, right, canvas, basis_sem, out_sem
):
    sector = lax.axis_index("sector")
    slab = lax.axis_index("slab")
    base_row = 2 * LINES * slab + LINES * sector
    width = TILE * TILE // BASIS_PARTS

    def basis_copy(part):
        columns = pl.ds(part * width, width)
        return pltpu.make_async_copy(
            basis_hbm.at[:, columns], basis.at[:, columns], basis_sem.at[part]
        )

    for part in range(BASIS_PARTS):
        basis_copy(part).start()
    canvas[...] = jnp.zeros_like(canvas)
    coeff = coeff_ref[:, :MODES].astype(BF16)
    rows_at = TILE // BASIS_PARTS
    for part in range(BASIS_PARTS):
        basis_copy(part).wait()
        outer = 0 if part < BASIS_PARTS // 2 else 2
        mix = jnp.concatenate([coeff[32 * outer : 32 * outer + 32], coeff[32:64]], axis=0)

        @pl.loop(0, rows_at // 4)
        def _(step):
            row = part * rows_at + step * 4
            columns = pl.ds(pl.multiple_of(row * TILE, 4 * TILE), 4 * TILE)
            phases = dot(mix, basis[:, columns])
            for extra in range(4):
                place = pl.ds(pl.multiple_of((row + extra + PAD) * 64, 64), 64)
                at = extra * TILE
                left[place, :] = phases[:, at : at + 128]
                right[place, :] = phases[:, at + 128 : at + 256]

    lane = lax.broadcasted_iota(jnp.int32, (1, 128), 1)
    down = lax.broadcasted_iota(jnp.int32, (HALF, 1), 0)
    reach = 7 * (TILE - 2)
    for part in range(LINES // HALF):
        rows = pl.ds(part * HALF, HALF)

        @pl.loop(0, NEAR)
        def _(slot):
            tile_row = slot_ref[slot, 1].astype(jnp.int32)
            column = slot_ref[slot, 2].astype(jnp.int32)
            weight = slot_ref[slot, 0] * slot_ref[slot, 3]
            top = part * HALF + base_row - tile_row
            inside = (top >= 17 - (HALF - 1)) & (top <= 238) & (slot_ref[slot, 3] > 0.0)

            @pl.when(inside)
            def _():
                held = lax.rem(slot, 64)
                block = column // 128
                shift = lax.rem(column, 128)
                start = (top + PAD) * 64 + held
                vertical = jnp.abs(2 * (top + down) - (TILE - 1))
                vertical = jnp.where(8 * vertical <= reach, 4 * vertical, 4 * reach)
                place = (lane - shift) & 127
                room_left = reach - 7 * ((TILE - 1) - 2 * place)
                room_right = reach - 7 * (2 * place + 1)
                fits_left = jnp.broadcast_to(vertical, (HALF, 128)) <= room_left
                fits_right = jnp.broadcast_to(vertical, (HALF, 128)) <= room_right
                wave = pltpu.roll(left[pl.ds(start, HALF, stride=64), :], shift, 1)
                left_cos, left_sin = circle(wave)
                wave = pltpu.roll(right[pl.ds(start, HALF, stride=64), :], shift, 1)
                right_cos, right_sin = circle(wave)
                kept = jnp.broadcast_to(lane >= shift, (HALF, 128))
                for comp, (one, two) in enumerate(
                    ((left_cos, right_cos), (left_sin, right_sin))
                ):
                    one = jnp.where(fits_left, one * weight, 0.0)
                    two = jnp.where(fits_right, two * weight, 0.0)
                    at = comp * (BLOCKS + 1) + block
                    canvas[at, rows, :] += jnp.where(kept, one, 0.0)
                    canvas[at + 1, rows, :] += jnp.where(kept, two, one)

                    @pl.when(shift > 0)
                    def _():
                        canvas[at + 2, rows, :] += jnp.where(kept, 0.0, two)

        for comp in range(2):
            pltpu.make_async_copy(
                canvas.at[pl.ds(comp * (BLOCKS + 1), BLOCKS), rows],
                field_hbm.at[pl.ds(comp * BLOCKS, BLOCKS), rows],
                out_sem.at[part, comp],
            ).start()
    for part in range(LINES // HALF):
        rows = pl.ds(part * HALF, HALF)
        for comp in range(2):
            pltpu.make_async_copy(
                canvas.at[pl.ds(comp * (BLOCKS + 1), BLOCKS), rows],
                field_hbm.at[pl.ds(comp * BLOCKS, BLOCKS), rows],
                out_sem.at[part, comp],
            ).wait()


def render(near, mode_basis):
    near = near.reshape(NEAR, 128)
    slots = near[:, MODES : MODES + 4]
    return pl.pallas_call(
        render_kernel,
        out_shape=jax.ShapeDtypeStruct((2 * BLOCKS, LINES, 128), F32),
        in_specs=[
            pl.BlockSpec(memory_space=pltpu.SMEM),
            pl.BlockSpec(memory_space=pltpu.VMEM),
            pl.BlockSpec(memory_space=pl.ANY),
        ],
        out_specs=pl.BlockSpec(memory_space=pl.ANY),
        scratch_shapes=[
            pltpu.VMEM((MODES, TILE * TILE), BF16),
            pltpu.VMEM(((TILE + 2 * PAD) * 64, 128), F32),
            pltpu.VMEM(((TILE + 2 * PAD) * 64, 128), F32),
            pltpu.VMEM((2 * (BLOCKS + 1) + 1, LINES, 128), F32),
            pltpu.SemaphoreType.DMA((BASIS_PARTS,)),
            pltpu.SemaphoreType.DMA((LINES // HALF, 2)),
        ],
        compiler_params=pltpu.CompilerParams(vmem_limit_bytes=44 << 20),
        name="render_rows",
    )(slots, near, mode_basis)


def encode(value):
    size = jnp.log(jnp.abs(value)) * (STEPS / math.log(2.0)) + (LOW * STEPS + 0.5)
    code = jnp.maximum(size, 0.0).astype(jnp.int32)
    return jnp.where(value < 0.0, -code, code)


def decode(code):
    size = jnp.abs(code).astype(F32) * (math.log(2.0) / STEPS) - LOW * math.log(2.0)
    value = jnp.exp(size)
    return jnp.where(code == 0, 0.0, jnp.where(code < 0, -value, value))


def exchange_kernel(
    field_hbm,
    col_first_both,
    col_first_low,
    col_twist,
    col_second,
    row_first,
    row_twist,
    mid_hbm,
    rows_in,
    wide,
    outbox,
    inbox,
    plain,
    staged,
    in_sem,
    send_sem,
    recv_sem,
    out_sem,
):
    sector = lax.axis_index("sector")
    slab = lax.axis_index("slab")
    me = sector * SLABS + slab
    source = 2 * slab + sector

    def fetch(chunk):
        return pltpu.make_async_copy(
            field_hbm.at[:, pl.ds(chunk * CHUNK, CHUNK)], rows_in.at[chunk], in_sem.at[chunk]
        )

    for chunk in range(CHUNKS):
        fetch(chunk).start()
    barrier = pltpu.get_barrier_semaphore()

    @pl.loop(1, DEVICES)
    def _(step):
        other = lax.rem(me + step, DEVICES)
        pl.semaphore_signal(
            barrier, inc=1, device_id=(other // SLABS, other % SLABS), device_id_type=MESH
        )

    for chunk in range(CHUNKS):
        fetch(chunk).wait()
        lines = rows_in.at[chunk].reshape(2 * BLOCKS * CHUNK, 128)
        codes = wide.reshape(DEVICES * CHUNK, 128)

        @pl.loop(0, CHUNK // 2)
        def _(step):
            both = jnp.concatenate(
                [lines[pl.ds(2 * step + e, 2 * BLOCKS, stride=CHUNK), :] for e in range(2)], axis=1
            )
            high, low = split(both)
            mid = dot(col_first_both[...], jnp.concatenate([high, low], axis=0))
            mid = mid + dot(col_first_low[...], high)
            highs, lows = [], []
            for e in range(2):
                real = mid[:64, 128 * e : 128 * e + 128]
                imag = mid[64:, 128 * e : 128 * e + 128]
                turned_real = real * col_twist[0] + imag * col_twist[1]
                turned_imag = imag * col_twist[0] - real * col_twist[1]
                real_high, real_low = split(turned_real)
                imag_high, imag_low = split(turned_imag)
                highs += [
                    jnp.concatenate([real_high, imag_high], axis=1),
                    jnp.concatenate([imag_high, -real_high], axis=1),
                ]
                lows += [
                    jnp.concatenate([real_low, imag_low], axis=1),
                    jnp.concatenate([imag_low, -real_low], axis=1),
                ]
            first = dot_lanes(col_second[...], jnp.concatenate(highs, axis=0))
            second = dot_lanes(col_second[:DEVICES, :], jnp.concatenate(lows, axis=0))
            done = encode(first[:DEVICES] + first[DEVICES:] + second)
            for e in range(2):
                codes[pl.ds(2 * step + e, DEVICES, stride=CHUNK), :] = done[
                    :, 128 * e : 128 * e + 128
                ]

        @pl.loop(0, DEVICES // 16)
        def _(step):
            some = pl.ds(step * 16, 16)
            outbox[chunk, some] = wide[some].astype(jnp.int16)

        if chunk == 0:
            pl.semaphore_wait(barrier, DEVICES - 1)

        @pl.loop(1, DEVICES)
        def _(step):
            other = lax.rem(me + step, DEVICES)
            pltpu.make_async_remote_copy(
                src_ref=outbox.at[chunk, other],
                dst_ref=inbox.at[chunk, source],
                send_sem=send_sem.at[chunk],
                recv_sem=recv_sem.at[chunk],
                device_id=(other // SLABS, other % SLABS),
                device_id_type=MESH,
            ).start()

        inbox[chunk, source] = outbox[chunk, me]

    def leave(chunk):
        return pltpu.make_async_copy(
            staged.at[chunk % 2],
            mid_hbm.at[:, pl.ds(chunk * CHUNK, CHUNK)],
            out_sem.at[chunk % 2],
        )

    for chunk in range(CHUNKS):
        most = inbox.at[chunk, pl.ds(0, DEVICES - 1)]
        pltpu.make_async_copy(most, most, recv_sem.at[chunk]).wait()
        if chunk >= 2:
            leave(chunk - 2).wait()

        @pl.loop(0, DEVICES // 16)
        def _(step):
            some = pl.ds(step * 16, 16)
            plain[some] = decode(inbox[chunk, some].astype(jnp.int32))

        values = plain.reshape(DEVICES * CHUNK, 128)

        @pl.loop(0, CHUNK // 4)
        def _(step):
            parts = []
            for e in range(4):
                turned = values[pl.ds(4 * step + e, DEVICES, stride=CHUNK), :].T
                parts.append(jnp.concatenate([turned[:64], turned[64:]], axis=1))
            high, low = split(jnp.concatenate(parts, axis=0))
            mid = dot(high, row_first[0]) + dot(high, row_first[1]) + dot(low, row_first[0])
            for e in range(4):
                line = pl.ds(chunk * CHUNK + 4 * step + e, 1)
                cos = row_twist[0, line, :]
                sin = row_twist[1, line, :]
                real = mid[64 * e : 64 * e + 64, :128]
                imag = mid[64 * e : 64 * e + 64, 128:]
                staged[chunk % 2, 0, 4 * step + e] = real * cos + imag * sin
                staged[chunk % 2, 1, 4 * step + e] = imag * cos - real * sin

        leave(chunk).start()

    for chunk in range(CHUNKS):
        most = outbox.at[chunk, pl.ds(0, DEVICES - 1)]
        pltpu.make_async_copy(most, most, send_sem.at[chunk]).wait()
    for chunk in range(CHUNKS - 2, CHUNKS):
        leave(chunk).wait()


def exchange(field, consts):
    vmem = pl.BlockSpec(memory_space=pltpu.VMEM)
    anywhere = pl.BlockSpec(memory_space=pl.ANY)
    return pl.pallas_call(
        exchange_kernel,
        out_shape=jax.ShapeDtypeStruct((2, LINES, LINES, 128), F32),
        in_specs=[anywhere] + [vmem] * len(consts),
        out_specs=anywhere,
        scratch_shapes=[
            pltpu.VMEM((CHUNKS, 2 * BLOCKS, CHUNK, 128), F32),
            pltpu.VMEM((DEVICES, CHUNK, 128), jnp.int32),
            pltpu.VMEM((CHUNKS, DEVICES, CHUNK, 128), jnp.int16),
            pltpu.VMEM((CHUNKS, DEVICES, CHUNK, 128), jnp.int16),
            pltpu.VMEM((DEVICES, CHUNK, 128), F32),
            pltpu.VMEM((2, 2, CHUNK, LINES, 128), F32),
            pltpu.SemaphoreType.DMA((CHUNKS,)),
            pltpu.SemaphoreType.DMA((CHUNKS,)),
            pltpu.SemaphoreType.DMA((CHUNKS,)),
            pltpu.SemaphoreType.DMA((2,)),
        ],
        compiler_params=pltpu.CompilerParams(
            collective_id=1, has_side_effects=True, vmem_limit_bytes=40 << 20
        ),
        name="exchange",
    )(field, *consts)


def finish_kernel(mid_ref, last_both, last_low, out_ref, turned):
    lines = mid_ref.reshape(2 * LINES * 8, 128)
    for pair in range(4):
        both = jnp.concatenate(
            [lines[pl.ds(2 * pair + e, 2 * LINES, stride=8), :] for e in range(2)], axis=1
        )
        high, low = split(both)
        done = dot(last_both[...], jnp.concatenate([high, low], axis=0))
        done = done + dot(last_low[...], high)
        for e in range(2):
            turned[pl.ds(2 * pair + e, 2 * LINES, stride=8), :] = done[:, 128 * e : 128 * e + 128]
    for comp in range(2):
        for block in range(LINES):
            at = (comp * LINES + block) * 8
            out_ref[comp, :, 128 * block : 128 * block + 128] = turned[at : at + 8, :]


def finish(mid, consts):
    return pl.pallas_call(
        finish_kernel,
        out_shape=jax.ShapeDtypeStruct((2, LINES, GRID), F32),
        grid=(LINES // 8,),
        in_specs=[
            pl.BlockSpec((2, LINES, 8, 128), lambda i: (0, 0, i, 0)),
            pl.BlockSpec((128, 256), lambda i: (0, 0)),
            pl.BlockSpec((128, 128), lambda i: (0, 0)),
        ],
        out_specs=pl.BlockSpec((2, 8, GRID), lambda i: (0, i, 0)),
        scratch_shapes=[pltpu.VMEM((2 * LINES * 8, 128), F32)],
        compiler_params=pltpu.CompilerParams(vmem_limit_bytes=24 << 20),
        name="finish",
    )(mid, *consts)


def body(mode_basis, mode_coeff, reflect, tile_row, tile_col, slot_live):
    scalars = jnp.stack([reflect.astype(F32), tile_row, tile_col, slot_live], axis=1)
    own = jnp.concatenate(
        [mode_coeff.astype(F32), scalars, jnp.zeros((SLOTS, 128 - MODES - 4), F32)], axis=1
    )
    first, last = tables()
    field = render(gather_near(own), mode_basis)
    mid = exchange(field, [jnp.asarray(t) for t in first])
    return finish(mid, [jnp.asarray(t) for t in last])


def solution(mesh):
    placed = (
        P(),
        P(("sector", "slab"), None),
        P(("sector", "slab")),
        P(("sector", "slab")),
        P(("sector", "slab")),
        P(("sector", "slab")),
    )
    return jax.shard_map(
        body,
        mesh=mesh,
        in_specs=placed,
        out_specs=P(None, ("sector", "slab"), None),
        check_vma=False,
    )
```

time: 874 us -> 90.3 us (0.10); the launches traced: 860 us -> 90 us
  waiting for transfers between devices: 317 us -> 0 us
  local copies, waits for them, and re-layouts: 271 us -> 3.41 us
  matrix products: 122 us -> 0 us
  Pallas kernels: 0 us -> 83.9 us
  loops' own time: 54.7 us -> 0 us
  other arithmetic: 54 us -> 2.63 us
  starting transfers between devices: 18.5 us -> 0 us
  between operations: 14.1 us -> 0.12 us
  blocking collectives: 9.32 us -> 0 us
    ppermute x2 -> x0, waiting for transfers between devices: 175 us -> none  [passed_along(): return lax.ppermute(block, axis, route)]
    dynamic_update_slice x32 -> x0, local copies, waits for them, and re-layouts: 105 us -> none  [deposit(): return lax.dynamic_update_slice(canvas, current + tile_piece, corner)]
    dot_general x24 -> x0, matrix products: 102 us -> none  [the longest x16 73.6 us: deposit(): jnp.dot(lax.dynamic_slice_in_dim(mode_coeff, slot_index, 1, 0), mode_basi...]
    unnamed x2 -> x0, waiting for transfers between devices: 89.6 us -> none
    pallas_call x0 -> x4, Pallas kernels: none -> 83.9 us  [the longest x1 43.5 us: exchange(): pl.pallas_call(exchange_kernel, out_shape=jax.ShapeDtypeStruct((2, LINES,...]
    dynamic_slice x96 -> x0, local copies, waits for them, and re-layouts: 62.5 us -> none  [the longest x32 24.9 us: deposit(): current = lax.dynamic_slice(canvas, corner, (2, tile_size, tile_size))]
    another operation x1 -> x0, loops' own time: 54.7 us -> none  [render(): return lax.fori_loop(0, mode_coeff.shape[0], deposit, canvas)]
    all_to_all x1 -> x0, waiting for transfers between devices: 52.2 us -> none  [body(): lax.all_to_all(along_cols, ('sector', 'slab'), split_axis=1, concat_axis=...]
  transfers between devices with their start and end apart: 4 -> 0, of which waited for: 4 -> 0; matrix products, arithmetic and copies ran while one was open for 0% -> 0% of each run, Pallas kernels for 0% -> 0%
where the time goes in v1:
time: 90.3 us; the launch traced here: 90 us
  Pallas kernels  83.9 us (93%)
  local copies, waits for them, and re-layouts  3.41 us (4%)
  other arithmetic  2.63 us (3%)
    pallas_call x1, Pallas kernels, exchange(): pl.pallas_call(exchange_kernel, out_shape=jax.ShapeDtypeStruct((2, LINES,...  43.5 us
    pallas_call x1, Pallas kernels, render(): pl.pallas_call(render_kernel, out_shape=jax.ShapeDtypeStruct((2 * BLOCKS,...  20.4 us
    pallas_call x1, Pallas kernels, gather_near(): pl.pallas_call(gather_kernel, out_shape=jax.ShapeDtypeStruct((3, 2, SLOTS...  14.5 us
    pallas_call x1, Pallas kernels, finish(): pl.pallas_call(finish_kernel, out_shape=jax.ShapeDtypeStruct((2, LINES, G...  5.51 us
    another operation x4, other arithmetic, body(): jnp.stack([reflect.astype(F32), tile_row, tile_col, slot_live], axis=1)  2.63 us

profile of v1, /device:TPU:1, one launch (start us, length us, event | category | flops | bytes accessed | tf_op | source)
XLA Modules:
  0.0 90.0 jit_solution(3894358190278378174)
XLA Ops:
  0.0 0.7 bitcast_convert_fusion
  0.7 0.7 convert_bitcast_fusion.2
  1.3 0.7 convert_bitcast_fusion.1
  2.0 0.7 convert_bitcast_fusion
  2.6 0.1 copy.17
  2.7 0.1 copy.16
  2.8 0.1 copy.15
  2.9 0.1 copy.14
  3.0 1.4 %concatenate.3.own_ref = f32[16,128]{1,0:T(8,128)} concatenate(bf16[16,64]{1,0:T(8,128)(2,1)} %param.14, f32[16,1]{1,0:T(8,128)S(1)} %copy.14, f32[16,1]{1,0:T(8,128)S(1)} %copy.15, f32[16,1]{1,0:T(8,128)S(1)} %copy.16, f32[16,1]{1,0:T(8,128)S(1)} %copy.17, f32[16,60]{1,0:T(8,128)S(1)} %broadcast_in_dim.3), dimensions={1} | concatenate | bytes 14336 | tf_op jit(solution)/shard_map/concatenate | solution.py:491
  4.3 14.5 %gather_near.1 = f32[3,2,16,128]{3,2,1,0:T(8,128)} custom-call(f32[16,128]{1,0:T(8,128)} %concatenate.3.own_ref), custom_call_target="tpu_custom_call" | custom-call | tf_op jit(solution)/shard_map/gather_near/pallas_call | solution.py:120
  18.8 0.9 slice.4.slot_ref
  19.7 0.8 copy-done
  20.5 0.0 copy-start.7
  20.5 20.4 %render_rows.1.field_hbm = f32[128,64,128]{2,1,0:T(8,128)S(1)} custom-call(f32[96,4]{1,0:T(8,128)S(1)} %slice.4.slot_ref, f32[96,128]{1,0:T(8,128)S(1)} %bitcast.11, bf16[64,65536]{1,0:T(8,128)(2,1)} %basis_hbm.1), custom_call_target="tpu_custom_call" | custom-call | tf_op jit(solution)/shard_map/render_rows/pallas_call | solution.py:248
  40.9 0.0 copy-done.1
  40.9 0.0 copy-done.2
  41.0 0.0 copy-done.3
  41.0 0.0 copy-done.5
  41.0 0.0 copy-done.7
  41.0 0.0 copy-start.4
  41.0 0.0 copy-start.6
  41.0 43.5 %exchange.1.mid_ref = f32[2,64,64,128]{3,2,1,0:T(8,128)S(1)} custom-call(f32[128,64,128]{2,1,0:T(8,128)S(1)} %render_rows.1.field_hbm, bf16[128,256]{1,0:T(8,128)(2,1)S(1)} %copy-done.5, bf16[128,128]{1,0:T(8,128)(2,1)S(1)} %copy-done.7, f32[2,64,128]{2,1,0:T(8,128)S(1)} %copy-done.1, bf16[256,256]{1,0:T(8,128)(2,1)S(1)} %copy-done.3, ...), custom_call_target="tpu_custom_call" | custom-call | tf_op jit(solution)/shard_map/exchange/pallas_call | solution.py:431
  84.5 0.0 copy-done.4
  84.5 5.5 %finish.1 = f32[2,64,8192]{2,1,0:T(8,128)} custom-call(f32[2,64,64,128]{3,2,1,0:T(8,128)S(1)} %exchange.1.mid_ref, bf16[128,256]{1,0:T(8,128)(2,1)S(1)} %copy-done.4, bf16[128,128]{1,0:T(8,128)(2,1)S(1)} %copy-done.6), custom_call_target="tpu_custom_call" | custom-call | tf_op jit(solution)/shard_map/finish/pallas_call | solution.py:473
  (7 shorter events, 0.0 us)
Async XLA Ops:
  19.7 0.8 copy-start
  20.5 20.5 %copy-start.1 = (f32[2,64,128]{2,1,0:T(8,128)S(1)}, f32[2,64,128]{2,1,0:T(8,128)}, u32[]{:S(2)}) copy-start(f32[2,64,128]{2,1,0:T(8,128)} %constant.18.clone.col_twist.row_twist) | copy-start | bytes 196612
  20.5 20.5 %copy-start.2 = (bf16[2,256,256]{2,1,0:T(8,128)(2,1)S(1)}, bf16[2,256,256]{2,1,0:T(8,128)(2,1)}, u32[]{:S(2)}) copy-start(bf16[2,256,256]{2,1,0:T(8,128)(2,1)} %constant.20.clone.row_first) | copy-start | bytes 786436
  20.5 20.5 %copy-start.3 = (bf16[256,256]{1,0:T(8,128)(2,1)S(1)}, bf16[256,256]{1,0:T(8,128)(2,1)}, u32[]{:S(2)}) copy-start(bf16[256,256]{1,0:T(8,128)(2,1)} %constant.19.clone.col_second) | copy-start | bytes 393220
  20.5 20.5 %copy-start.5 = (bf16[128,256]{1,0:T(8,128)(2,1)S(1)}, bf16[128,256]{1,0:T(8,128)(2,1)}, u32[]{:S(2)}) copy-start(bf16[128,256]{1,0:T(8,128)(2,1)} %constant.16.clone.col_first_both) | copy-start | bytes 196612
  20.5 20.5 %copy-start.7 = (bf16[128,128]{1,0:T(8,128)(2,1)S(1)}, bf16[128,128]{1,0:T(8,128)(2,1)}, u32[]{:S(2)}) copy-start(bf16[128,128]{1,0:T(8,128)(2,1)} %constant.17.clone.col_first_low) | copy-start | bytes 98308
  41.0 43.5 %copy-start.4 = (bf16[128,256]{1,0:T(8,128)(2,1)S(1)}, bf16[128,256]{1,0:T(8,128)(2,1)}, u32[]{:S(2)}) copy-start(bf16[128,256]{1,0:T(8,128)(2,1)} %constant.21.clone.last_both) | copy-start | bytes 196612
  41.0 43.5 %copy-start.6 = (bf16[128,128]{1,0:T(8,128)(2,1)S(1)}, bf16[128,128]{1,0:T(8,128)(2,1)}, u32[]{:S(2)}) copy-start(bf16[128,128]{1,0:T(8,128)(2,1)} %constant.22.clone.last_low) | copy-start | bytes 98308

commit v2 on v1

--- a/solution.py
+++ b/solution.py
@@ -60,14 +60,13 @@
     twist = angles(64, 128, GRID)
     col_twist = np.stack([np.cos(twist), np.sin(twist)]).astype(np.float32)
     second = angles(128, 128, 128)
-    col_second = np.concatenate(halves(np.concatenate([np.cos(second), np.sin(second)], axis=1)))
     row_first = np.stack(
         halves(np.block([[np.cos(second), -np.sin(second)], [np.sin(second), np.cos(second)]]))
     )
     last_high, last_low = halves(col_first / GRID)
     last_both = np.concatenate([last_high, last_high], axis=1)
     return (
-        (col_first_both, low, col_twist, col_second, row_first, col_twist),
+        (col_first_both, low, col_twist, row_first, col_twist),
         (last_both, last_low),
     )
 
@@ -81,11 +80,9 @@
     return jnp.dot(left, right, preferred_element_type=F32)
 
 
-def dot_lanes(left, right):
-    return lax.dot_general(left, right, (((1,), (1,)), ((), ())), preferred_element_type=F32)
-
-
-def gather_kernel(own_ref, near_ref, send_sem, recv_sem):
+def gather_kernel(
+    coeff_ref, reflect_ref, row_ref, column_ref, live_ref, near_ref, own, own_sem, send_sem, recv_sem
+):
     sector = lax.axis_index("sector")
     slab = lax.axis_index("slab")
     barrier = pltpu.get_barrier_semaphore()
@@ -98,12 +95,16 @@
                 device_id=(lax.rem(sector + flip, 2), lax.rem(slab + step + SLABS, SLABS)),
                 device_id_type=MESH,
             )
-    near_ref[0, sector] = own_ref[...]
+    own[:SLOTS, :MODES] = coeff_ref[...].astype(F32)
+    for number, ref in enumerate((reflect_ref, row_ref, column_ref, live_ref)):
+        own[SLOTS + number : SLOTS + number + 1, :SLOTS] = ref[...].astype(F32)
+    kept = pltpu.make_async_copy(own, near_ref.at[0, sector], own_sem)
+    kept.start()
     pl.semaphore_wait(barrier, 9)
     copies = []
     for number, (flip, hop) in enumerate(others):
         copy = pltpu.make_async_remote_copy(
-            src_ref=own_ref,
+            src_ref=own,
             dst_ref=near_ref.at[hop, sector],
             send_sem=send_sem.at[number],
             recv_sem=recv_sem.at[number],
@@ -112,20 +113,27 @@
         )
         copy.start()
         copies.append(copy)
+    kept.wait()
     for copy in copies:
         copy.wait()
 
 
-def gather_near(own):
+def gather_near(mode_coeff, *lists):
+    vmem = pl.BlockSpec(memory_space=pltpu.VMEM)
     return pl.pallas_call(
         gather_kernel,
-        out_shape=jax.ShapeDtypeStruct((3, 2, SLOTS, 128), F32),
-        in_specs=[pl.BlockSpec(memory_space=pltpu.VMEM)],
-        out_specs=pl.BlockSpec(memory_space=pltpu.VMEM),
-        scratch_shapes=[pltpu.SemaphoreType.DMA((5,)), pltpu.SemaphoreType.DMA((5,))],
+        out_shape=jax.ShapeDtypeStruct((3, 2, SLOTS + 8, 128), F32),
+        in_specs=[vmem] * 5,
+        out_specs=pl.BlockSpec(memory_space=pl.ANY),
+        scratch_shapes=[
+            pltpu.VMEM((SLOTS + 8, 128), F32),
+            pltpu.SemaphoreType.DMA,
+            pltpu.SemaphoreType.DMA((5,)),
+            pltpu.SemaphoreType.DMA((5,)),
+        ],
         compiler_params=pltpu.CompilerParams(collective_id=0, has_side_effects=True),
         name="gather_near",
-    )(own)
+    )(mode_coeff, *(values.reshape(1, SLOTS) for values in lists))
 
 
 def circle(phase):
@@ -144,10 +152,24 @@
 
 
 BASIS_PARTS = 8
+TOGETHER = 8
 
 
 def render_kernel(
-    slot_ref, coeff_ref, basis_hbm, field_hbm, basis, left, right, canvas, basis_sem, out_sem
+    near_hbm,
+    basis_hbm,
+    field_hbm,
+    near,
+    basis,
+    left,
+    right,
+    canvas,
+    slots,
+    tasks,
+    near_sem,
+    slots_sem,
+    basis_sem,
+    out_sem,
 ):
     sector = lax.axis_index("sector")
     slab = lax.axis_index("slab")
@@ -160,22 +182,49 @@
             basis_hbm.at[:, columns], basis.at[:, columns], basis_sem.at[part]
         )
 
+    near_copy = pltpu.make_async_copy(near_hbm, near, near_sem)
+    slots_copy = pltpu.make_async_copy(near_hbm.at[:, :, pl.ds(SLOTS, 8)], slots, slots_sem)
+    slots_copy.start()
+    near_copy.start()
     for part in range(BASIS_PARTS):
         basis_copy(part).start()
     canvas[...] = jnp.zeros_like(canvas)
-    coeff = coeff_ref[:, :MODES].astype(BF16)
+    slots_copy.wait()
+
+    def about(slot):
+        hop = slot // (2 * SLOTS)
+        side = slot // SLOTS % 2
+        at = slot % SLOTS
+        return [slots[hop, side, number, at] for number in range(4)]
+
+    def collect(slot, counts):
+        _, tile_row, _, live = about(slot)
+        top = base_row - tile_row.astype(jnp.int32)
+        found = []
+        for part, count in enumerate(counts):
+            start = top + part * HALF
+            reaches = (start >= 17 - (HALF - 1)) & (start <= 238) & (live > 0.0)
+            tasks[part, count] = slot
+            found.append(count + reaches.astype(jnp.int32))
+        return tuple(found)
+
+    counts = lax.fori_loop(0, NEAR, collect, (0,) * (LINES // HALF))
+    near_copy.wait()
+    coeff = [
+        jnp.concatenate([near[hop, side, :SLOTS, :MODES] for side in range(2)], axis=0).astype(BF16)
+        for hop in range(3)
+    ]
     rows_at = TILE // BASIS_PARTS
     for part in range(BASIS_PARTS):
         basis_copy(part).wait()
-        outer = 0 if part < BASIS_PARTS // 2 else 2
-        mix = jnp.concatenate([coeff[32 * outer : 32 * outer + 32], coeff[32:64]], axis=0)
-
-        @pl.loop(0, rows_at // 4)
-        def _(step):
-            row = part * rows_at + step * 4
-            columns = pl.ds(pl.multiple_of(row * TILE, 4 * TILE), 4 * TILE)
+        mix = jnp.concatenate([coeff[0 if part < BASIS_PARTS // 2 else 2], coeff[1]], axis=0)
+
+        @pl.loop(0, rows_at // TOGETHER)
+        def _(step):
+            row = part * rows_at + step * TOGETHER
+            columns = pl.ds(pl.multiple_of(row * TILE, TOGETHER * TILE), TOGETHER * TILE)
             phases = dot(mix, basis[:, columns])
-            for extra in range(4):
+            for extra in range(TOGETHER):
                 place = pl.ds(pl.multiple_of((row + extra + PAD) * 64, 64), 64)
                 at = extra * TILE
                 left[place, :] = phases[:, at : at + 128]
@@ -184,47 +233,52 @@
     lane = lax.broadcasted_iota(jnp.int32, (1, 128), 1)
     down = lax.broadcasted_iota(jnp.int32, (HALF, 1), 0)
     reach = 7 * (TILE - 2)
+
+    def tile_part(slot, part, counted):
+        reflectivity, tile_row, column, live = about(slot)
+        weight = jnp.where(counted, reflectivity * live, 0.0)
+        column = column.astype(jnp.int32)
+        top = part * HALF + base_row - tile_row.astype(jnp.int32)
+        block = column // 128
+        shift = lax.rem(column, 128)
+        start = (top + PAD) * 64 + lax.rem(slot, 64)
+        vertical = jnp.abs(2 * (top + down) - (TILE - 1))
+        vertical = jnp.where(8 * vertical <= reach, 4 * vertical, 4 * reach)
+        vertical = jnp.broadcast_to(vertical, (HALF, 128))
+        place = (lane - shift) & 127
+        room_left = reach - 7 * ((TILE - 1) - 2 * place)
+        room_right = reach - 7 * (2 * place + 1)
+        both = []
+        for ref, room in ((left, room_left), (right, room_right)):
+            wave = pltpu.roll(ref[pl.ds(start, HALF, stride=64), :], shift, 1)
+            amplitude = jnp.where(vertical <= room, weight, 0.0)
+            inside = amplitude > 0.0
+            cosine, sine = circle(wave)
+            both.append(
+                (
+                    jnp.where(inside, cosine * amplitude, 0.0),
+                    jnp.where(inside, sine * amplitude, 0.0),
+                )
+            )
+        return block, jnp.broadcast_to(lane >= shift, (HALF, 128)), both
+
     for part in range(LINES // HALF):
         rows = pl.ds(part * HALF, HALF)
-
-        @pl.loop(0, NEAR)
-        def _(slot):
-            tile_row = slot_ref[slot, 1].astype(jnp.int32)
-            column = slot_ref[slot, 2].astype(jnp.int32)
-            weight = slot_ref[slot, 0] * slot_ref[slot, 3]
-            top = part * HALF + base_row - tile_row
-            inside = (top >= 17 - (HALF - 1)) & (top <= 238) & (slot_ref[slot, 3] > 0.0)
-
-            @pl.when(inside)
-            def _():
-                held = lax.rem(slot, 64)
-                block = column // 128
-                shift = lax.rem(column, 128)
-                start = (top + PAD) * 64 + held
-                vertical = jnp.abs(2 * (top + down) - (TILE - 1))
-                vertical = jnp.where(8 * vertical <= reach, 4 * vertical, 4 * reach)
-                place = (lane - shift) & 127
-                room_left = reach - 7 * ((TILE - 1) - 2 * place)
-                room_right = reach - 7 * (2 * place + 1)
-                fits_left = jnp.broadcast_to(vertical, (HALF, 128)) <= room_left
-                fits_right = jnp.broadcast_to(vertical, (HALF, 128)) <= room_right
-                wave = pltpu.roll(left[pl.ds(start, HALF, stride=64), :], shift, 1)
-                left_cos, left_sin = circle(wave)
-                wave = pltpu.roll(right[pl.ds(start, HALF, stride=64), :], shift, 1)
-                right_cos, right_sin = circle(wave)
-                kept = jnp.broadcast_to(lane >= shift, (HALF, 128))
-                for comp, (one, two) in enumerate(
-                    ((left_cos, right_cos), (left_sin, right_sin))
-                ):
-                    one = jnp.where(fits_left, one * weight, 0.0)
-                    two = jnp.where(fits_right, two * weight, 0.0)
+        count = counts[part]
+
+        @pl.loop(0, (count + 1) // 2)
+        def _(step):
+            pieces = []
+            for extra in range(2):
+                at = 2 * step + extra
+                pieces.append(tile_part(tasks[part, jnp.minimum(at, count - 1)], part, at < count))
+            for block, kept, both in pieces:
+                for comp in range(2):
+                    one, two = both[0][comp], both[1][comp]
                     at = comp * (BLOCKS + 1) + block
                     canvas[at, rows, :] += jnp.where(kept, one, 0.0)
                     canvas[at + 1, rows, :] += jnp.where(kept, two, one)
-
-                    @pl.when(shift > 0)
-                    def _():
-                        canvas[at + 2, rows, :] += jnp.where(kept, 0.0, two)
+                    canvas[at + 2, rows, :] += jnp.where(kept, 0.0, two)
 
         for comp in range(2):
             pltpu.make_async_copy(
@@ -243,28 +297,28 @@
 
 
 def render(near, mode_basis):
-    near = near.reshape(NEAR, 128)
-    slots = near[:, MODES : MODES + 4]
+    anywhere = pl.BlockSpec(memory_space=pl.ANY)
     return pl.pallas_call(
         render_kernel,
         out_shape=jax.ShapeDtypeStruct((2 * BLOCKS, LINES, 128), F32),
-        in_specs=[
-            pl.BlockSpec(memory_space=pltpu.SMEM),
-            pl.BlockSpec(memory_space=pltpu.VMEM),
-            pl.BlockSpec(memory_space=pl.ANY),
-        ],
-        out_specs=pl.BlockSpec(memory_space=pl.ANY),
+        in_specs=[anywhere, anywhere],
+        out_specs=anywhere,
         scratch_shapes=[
+            pltpu.VMEM((3, 2, SLOTS + 8, 128), F32),
             pltpu.VMEM((MODES, TILE * TILE), BF16),
             pltpu.VMEM(((TILE + 2 * PAD) * 64, 128), F32),
             pltpu.VMEM(((TILE + 2 * PAD) * 64, 128), F32),
-            pltpu.VMEM((2 * (BLOCKS + 1) + 1, LINES, 128), F32),
+            pltpu.VMEM((2 * (BLOCKS + 1), LINES, 128), F32),
+            pltpu.SMEM((3, 2, 8, 128), F32),
+            pltpu.SMEM((LINES // HALF, NEAR), jnp.int32),
+            pltpu.SemaphoreType.DMA,
+            pltpu.SemaphoreType.DMA,
             pltpu.SemaphoreType.DMA((BASIS_PARTS,)),
             pltpu.SemaphoreType.DMA((LINES // HALF, 2)),
         ],
         compiler_params=pltpu.CompilerParams(vmem_limit_bytes=44 << 20),
         name="render_rows",
-    )(slots, near, mode_basis)
+    )(near, mode_basis)
 
 
 def encode(value):
@@ -284,7 +338,6 @@
     col_first_both,
     col_first_low,
     col_twist,
-    col_second,
     row_first,
     row_twist,
     mid_hbm,
@@ -325,37 +378,33 @@
         lines = rows_in.at[chunk].reshape(2 * BLOCKS * CHUNK, 128)
         codes = wide.reshape(DEVICES * CHUNK, 128)
 
-        @pl.loop(0, CHUNK // 2)
-        def _(step):
-            both = jnp.concatenate(
-                [lines[pl.ds(2 * step + e, 2 * BLOCKS, stride=CHUNK), :] for e in range(2)], axis=1
-            )
-            high, low = split(both)
-            mid = dot(col_first_both[...], jnp.concatenate([high, low], axis=0))
-            mid = mid + dot(col_first_low[...], high)
-            highs, lows = [], []
-            for e in range(2):
-                real = mid[:64, 128 * e : 128 * e + 128]
-                imag = mid[64:, 128 * e : 128 * e + 128]
-                turned_real = real * col_twist[0] + imag * col_twist[1]
-                turned_imag = imag * col_twist[0] - real * col_twist[1]
-                real_high, real_low = split(turned_real)
-                imag_high, imag_low = split(turned_imag)
-                highs += [
-                    jnp.concatenate([real_high, imag_high], axis=1),
-                    jnp.concatenate([imag_high, -real_high], axis=1),
-                ]
-                lows += [
-                    jnp.concatenate([real_low, imag_low], axis=1),
-                    jnp.concatenate([imag_low, -real_low], axis=1),
-                ]
-            first = dot_lanes(col_second[...], jnp.concatenate(highs, axis=0))
-            second = dot_lanes(col_second[:DEVICES, :], jnp.concatenate(lows, axis=0))
-            done = encode(first[:DEVICES] + first[DEVICES:] + second)
-            for e in range(2):
-                codes[pl.ds(2 * step + e, DEVICES, stride=CHUNK), :] = done[
-                    :, 128 * e : 128 * e + 128
-                ]
+        @pl.loop(0, CHUNK // 4)
+        def _(step):
+            parts = []
+            for pair in range(2):
+                both = jnp.concatenate(
+                    [
+                        lines[pl.ds(4 * step + 2 * pair + e, 2 * BLOCKS, stride=CHUNK), :]
+                        for e in range(2)
+                    ],
+                    axis=1,
+                )
+                high, low = split(both)
+                mid = dot(col_first_both[...], jnp.concatenate([high, low], axis=0))
+                mid = mid + dot(col_first_low[...], high)
+                for e in range(2):
+                    real = mid[:64, 128 * e : 128 * e + 128]
+                    imag = mid[64:, 128 * e : 128 * e + 128]
+                    turned_real = real * col_twist[0] + imag * col_twist[1]
+                    turned_imag = imag * col_twist[0] - real * col_twist[1]
+                    parts.append(jnp.concatenate([turned_real, turned_imag], axis=1))
+            high, low = split(jnp.concatenate(parts, axis=0))
+            done = dot(high, row_first[0]) + dot(high, row_first[1]) + dot(low, row_first[0])
+            done = encode(done)
+            for e in range(4):
+                some = done[64 * e : 64 * e + 64]
+                some = jnp.concatenate([some[:, :128], some[:, 128:]], axis=0).T
+                codes[pl.ds(4 * step + e, DEVICES, stride=CHUNK), :] = some
 
         @pl.loop(0, DEVICES // 16)
         def _(step):
@@ -487,12 +536,9 @@
 
 
 def body(mode_basis, mode_coeff, reflect, tile_row, tile_col, slot_live):
-    scalars = jnp.stack([reflect.astype(F32), tile_row, tile_col, slot_live], axis=1)
-    own = jnp.concatenate(
-        [mode_coeff.astype(F32), scalars, jnp.zeros((SLOTS, 128 - MODES - 4), F32)], axis=1
-    )
     first, last = tables()
-    field = render(gather_near(own), mode_basis)
+    near = gather_near(mode_coeff, reflect, tile_row, tile_col, slot_live)
+    field = render(near, mode_basis)
     mid = exchange(field, [jnp.asarray(t) for t in first])
     return finish(mid, [jnp.asarray(t) for t in last])
 

time: 90.3 us -> 72.5 us (0.80)
  Pallas kernels: 83.9 us -> 71.2 us
  other arithmetic: 2.63 us -> 0 us
  local copies, waits for them, and re-layouts: 3.41 us -> 0.91 us
    pallas_call x1, Pallas kernels: 20.4 us -> 13.5 us  [render(): pl.pallas_call(render_kernel, out_shape=jax.ShapeDtypeStruct((2 * BLOCKS,...]
    pallas_call x1, Pallas kernels: 43.5 us -> 38.1 us  [exchange(): pl.pallas_call(exchange_kernel, out_shape=jax.ShapeDtypeStruct((2, LINES,...]
    another operation x4 -> x0, other arithmetic: 2.63 us -> none  [body(): jnp.stack([reflect.astype(F32), tile_row, tile_col, slot_live], axis=1)]
    concatenate x1 -> x0, local copies, waits for them, and re-layouts: 1.36 us -> none  [body(): jnp.concatenate([mode_coeff.astype(F32), scalars, jnp.zeros((SLOTS, 128 -...]
where the time goes in v2:
time: 72.5 us; the launch traced here: 72.2 us
  Pallas kernels  71.2 us (98%)
  local copies, waits for them, and re-layouts  0.91 us (1%)
    pallas_call x1, Pallas kernels, exchange(): pl.pallas_call(exchange_kernel, out_shape=jax.ShapeDtypeStruct((2, LINES,...  38.1 us
    pallas_call x1, Pallas kernels, gather_near(): pl.pallas_call(gather_kernel, out_shape=jax.ShapeDtypeStruct((3, 2, SLOTS...  14.1 us
    pallas_call x1, Pallas kernels, render(): pl.pallas_call(render_kernel, out_shape=jax.ShapeDtypeStruct((2 * BLOCKS,...  13.5 us
    pallas_call x1, Pallas kernels, finish(): pl.pallas_call(finish_kernel, out_shape=jax.ShapeDtypeStruct((2, LINES, G...  5.52 us

profile of v2, /device:TPU:1, one launch (start us, length us, event | category | flops | bytes accessed | tf_op | source)
XLA Modules:
  0.0 72.2 jit_solution(13485668711721942263)
XLA Ops:
  0.0 14.1 %gather_near.1.near_hbm = f32[3,2,24,128]{3,2,1,0:T(8,128)} custom-call(bf16[16,64]{1,0:T(8,128)(2,1)} %coeff_ref.1, bf16[1,16]{1,0:T(2,128)(2,1)} %bitcast.4, s32[1,16]{1,0:T(1,128)} %bitcast.5, s32[1,16]{1,0:T(1,128)} %bitcast.6, s32[1,16]{1,0:T(1,128)} %bitcast.7), custom_call_target="tpu_custom_call" | custom-call | tf_op jit(solution)/shard_map/gather_near/pallas_call | solution.py:123
  14.1 0.0 copy-start
  14.1 0.9 %copy-done = f32[3,2,24,128]{3,2,1,0:T(8,128)S(1)} copy-done((f32[3,2,24,128]{3,2,1,0:T(8,128)S(1)}, f32[3,2,24,128]{3,2,1,0:T(8,128)}, u32[]{:S(2)}) %copy-start) | copy-done | bytes 73752
  15.0 0.0 copy-start.1
  15.0 0.0 copy-start.2
  15.0 0.0 copy-start.4
  15.0 0.0 copy-start.6
  15.0 13.5 %render_rows.1.field_hbm = f32[128,64,128]{2,1,0:T(8,128)S(1)} custom-call(f32[3,2,24,128]{3,2,1,0:T(8,128)S(1)} %copy-done, bf16[64,65536]{1,0:T(8,128)(2,1)} %basis_hbm.1), custom_call_target="tpu_custom_call" | custom-call | tf_op jit(solution)/shard_map/render_rows/pallas_call | solution.py:301
  28.6 0.0 copy-done.1
  28.6 0.0 copy-done.2
  28.6 0.0 copy-done.4
  28.6 0.0 copy-done.6
  28.6 0.0 copy-start.3
  28.6 0.0 copy-start.5
  28.6 38.1 %exchange.1.mid_ref = f32[2,64,64,128]{3,2,1,0:T(8,128)S(1)} custom-call(f32[128,64,128]{2,1,0:T(8,128)S(1)} %render_rows.1.field_hbm, bf16[128,256]{1,0:T(8,128)(2,1)S(1)} %copy-done.4, bf16[128,128]{1,0:T(8,128)(2,1)S(1)} %copy-done.6, f32[2,64,128]{2,1,0:T(8,128)S(1)} %copy-done.1, bf16[2,256,256]{2,1,0:T(8,128)(2,1)S(1)} %copy-done.2, ...), custom_call_target="tpu_custom_call" | custom-call | tf_op jit(solution)/shard_map/exchange/pallas_call | solution.py:480
  66.7 0.0 copy-done.3
  66.7 0.0 copy-done.5
  66.7 5.5 %finish.1 = f32[2,64,8192]{2,1,0:T(8,128)} custom-call(f32[2,64,64,128]{3,2,1,0:T(8,128)S(1)} %exchange.1.mid_ref, bf16[128,256]{1,0:T(8,128)(2,1)S(1)} %copy-done.3, bf16[128,128]{1,0:T(8,128)(2,1)S(1)} %copy-done.5), custom_call_target="tpu_custom_call" | custom-call | tf_op jit(solution)/shard_map/finish/pallas_call | solution.py:522
Async XLA Ops:
  14.1 0.9 %copy-start = (f32[3,2,24,128]{3,2,1,0:T(8,128)S(1)}, f32[3,2,24,128]{3,2,1,0:T(8,128)}, u32[]{:S(2)}) copy-start(f32[3,2,24,128]{3,2,1,0:T(8,128)} %gather_near.1.near_hbm) | copy-start | bytes 221188
  15.0 13.6 %copy-start.1 = (f32[2,64,128]{2,1,0:T(8,128)S(1)}, f32[2,64,128]{2,1,0:T(8,128)}, u32[]{:S(2)}) copy-start(f32[2,64,128]{2,1,0:T(8,128)} %constant.14.clone.col_twist.row_twist) | copy-start | bytes 196612
  15.0 13.6 %copy-start.2 = (bf16[2,256,256]{2,1,0:T(8,128)(2,1)S(1)}, bf16[2,256,256]{2,1,0:T(8,128)(2,1)}, u32[]{:S(2)}) copy-start(bf16[2,256,256]{2,1,0:T(8,128)(2,1)} %constant.15.clone.row_first) | copy-start | bytes 786436
  15.0 13.6 %copy-start.4 = (bf16[128,256]{1,0:T(8,128)(2,1)S(1)}, bf16[128,256]{1,0:T(8,128)(2,1)}, u32[]{:S(2)}) copy-start(bf16[128,256]{1,0:T(8,128)(2,1)} %constant.12.clone.col_first_both) | copy-start | bytes 196612
  15.0 13.6 %copy-start.6 = (bf16[128,128]{1,0:T(8,128)(2,1)S(1)}, bf16[128,128]{1,0:T(8,128)(2,1)}, u32[]{:S(2)}) copy-start(bf16[128,128]{1,0:T(8,128)(2,1)} %constant.13.clone.col_first_low) | copy-start | bytes 98308
  28.6 38.1 %copy-start.3 = (bf16[128,256]{1,0:T(8,128)(2,1)S(1)}, bf16[128,256]{1,0:T(8,128)(2,1)}, u32[]{:S(2)}) copy-start(bf16[128,256]{1,0:T(8,128)(2,1)} %constant.16.clone.last_both) | copy-start | bytes 196612
  28.6 38.1 %copy-start.5 = (bf16[128,128]{1,0:T(8,128)(2,1)S(1)}, bf16[128,128]{1,0:T(8,128)(2,1)}, u32[]{:S(2)}) copy-start(bf16[128,128]{1,0:T(8,128)(2,1)} %constant.17.clone.last_low) | copy-start | bytes 98308

commit v3 on v2

v3 whole, which is shorter than its diff:
```python
import functools
import math

import jax
import jax.numpy as jnp
import ml_dtypes
import numpy as np
from jax import lax
from jax.experimental import pallas as pl
from jax.experimental.pallas import tpu as pltpu
from jax.sharding import PartitionSpec as P

GRID = 8192
TILE = 256
SLOTS = 16
MODES = 64
SLABS = 64
DEVICES = 128
LINES = GRID // DEVICES
BLOCKS = GRID // 128
NEAR = 6 * SLOTS
CHUNK = 16
CHUNKS = LINES // CHUNK
PAD = 16
HALF = 32
MESH = pl.DeviceIdType.MESH
F32 = jnp.float32
BF16 = jnp.bfloat16

LOW = 12.0
STEPS = 32766.0 / (LOW + 15.25)


def polynomial(values, powers):
    spots = np.cos(np.pi * (np.arange(400) + 0.5) / 800) * 0.5
    table = np.stack([spots**power for power in powers], axis=1)
    return [float(c) for c in np.linalg.lstsq(table, values(np.pi * spots), rcond=None)[0]]


SIN_TERMS = polynomial(np.sin, (1, 3, 5, 7))
COS_TERMS = polynomial(np.cos, (0, 2, 4, 6))


def halves(table):
    high = table.astype(ml_dtypes.bfloat16)
    low = (table - high.astype(np.float64)).astype(ml_dtypes.bfloat16)
    return high, low


def angles(left, right, total):
    turns = np.outer(np.arange(left), np.arange(right)) % total
    return 2.0 * math.pi * turns / total


def stacked(table):
    high, low = halves(table)
    return np.block([[high, high], [low, np.zeros_like(low)]])


def tables():
    first = angles(64, 64, 64)
    turn = np.block([[np.cos(first), np.sin(first)], [-np.sin(first), np.cos(first)]])
    twist = angles(64, 128, GRID)
    second = angles(128, 128, 128)
    long_turn = np.block([[np.cos(second), -np.sin(second)], [np.sin(second), np.cos(second)]])
    return (
        stacked(turn),
        np.stack([np.cos(twist), np.sin(twist)]).astype(np.float32),
        np.stack(halves(long_turn)),
        stacked(turn / GRID),
    )


def split(value):
    high = value.astype(BF16)
    return high, (value - high.astype(F32)).astype(BF16)


def dot(left, right):
    return jnp.dot(left, right, preferred_element_type=F32)


def dot_short(table, value):
    high, low = split(value)
    both = dot(table, jnp.concatenate([high, low], axis=0))
    return both[:128] + both[128:]


def dot_long(value, tables):
    high, low = split(value)
    return dot(high, tables[0]) + dot(high, tables[1]) + dot(low, tables[0])


def gather_kernel(
    basis_hbm,
    coeff_hbm,
    reflect_hbm,
    row_hbm,
    column_hbm,
    live_hbm,
    near_ref,
    basis_ref,
    coeff_ref,
    reflect_ref,
    row_ref,
    column_ref,
    live_ref,
    own,
    basis_sem,
    in_sem,
    send_sem,
    recv_sem,
):
    sector = lax.axis_index("sector")
    slab = lax.axis_index("slab")
    barrier = pltpu.get_barrier_semaphore()
    sources = (coeff_hbm, reflect_hbm, row_hbm, column_hbm, live_hbm)
    held = (coeff_ref, reflect_ref, row_ref, column_ref, live_ref)
    loads = [
        pltpu.make_async_copy(one, two, in_sem.at[number])
        for number, (one, two) in enumerate(zip(sources, held))
    ]
    for load in loads:
        load.start()
    others = [(flip, hop) for hop in range(3) for flip in range(2)][1:]
    for flip, hop in others:
        for step in {hop, -hop}:
            pl.semaphore_signal(
                barrier,
                inc=1,
                device_id=(lax.rem(sector + flip, 2), lax.rem(slab + step + SLABS, SLABS)),
                device_id_type=MESH,
            )
    basis_copy = pltpu.make_async_copy(basis_hbm, basis_ref, basis_sem)
    basis_copy.start()
    for load in loads:
        load.wait()
    own[:SLOTS, :MODES] = coeff_ref[...].astype(F32)
    for number, ref in enumerate((reflect_ref, row_ref, column_ref, live_ref)):
        own[SLOTS + number : SLOTS + number + 1, :SLOTS] = ref[...].astype(F32)
    near_ref[0, sector] = own[...]
    pl.semaphore_wait(barrier, 9)
    copies = []
    for number, (flip, hop) in enumerate(others):
        copy = pltpu.make_async_remote_copy(
            src_ref=own,
            dst_ref=near_ref.at[hop, sector],
            send_sem=send_sem.at[number],
            recv_sem=recv_sem.at[number],
            device_id=(lax.rem(sector + flip, 2), lax.rem(slab + hop, SLABS)),
            device_id_type=MESH,
        )
        copy.start()
        copies.append(copy)
    for copy in copies:
        copy.wait()
    basis_copy.wait()


def gather_near(mode_basis, mode_coeff, *lists):
    vmem = pl.BlockSpec(memory_space=pltpu.VMEM)
    values = [mode_basis, mode_coeff] + [one.reshape(1, SLOTS) for one in lists]
    return pl.pallas_call(
        gather_kernel,
        out_shape=[
            jax.ShapeDtypeStruct((3, 2, SLOTS + 8, 128), F32),
            jax.ShapeDtypeStruct(mode_basis.shape, BF16),
        ],
        in_specs=[pl.BlockSpec(memory_space=pltpu.HBM)] * 6,
        out_specs=[vmem, vmem],
        scratch_shapes=[
            pltpu.VMEM((SLOTS, MODES), BF16),
            pltpu.VMEM((1, SLOTS), BF16),
            pltpu.VMEM((1, SLOTS), jnp.int32),
            pltpu.VMEM((1, SLOTS), jnp.int32),
            pltpu.VMEM((1, SLOTS), jnp.int32),
            pltpu.VMEM((SLOTS + 8, 128), F32),
            pltpu.SemaphoreType.DMA,
            pltpu.SemaphoreType.DMA((5,)),
            pltpu.SemaphoreType.DMA((5,)),
            pltpu.SemaphoreType.DMA((5,)),
        ],
        compiler_params=pltpu.CompilerParams(
            collective_id=0, has_side_effects=True, vmem_limit_bytes=20 << 20
        ),
        name="gather_near",
    )(*(pltpu.with_memory_space_constraint(value, pltpu.HBM) for value in values))


def circle(phase):
    turns = phase * (0.5 / math.pi)
    part = turns - jnp.round(turns)
    square = part * part
    sine = SIN_TERMS[-1]
    for term in SIN_TERMS[-2::-1]:
        sine = sine * square + term
    sine = sine * part
    cosine = COS_TERMS[-1]
    for term in COS_TERMS[-2::-1]:
        cosine = cosine * square + term
    double = sine + sine
    return 1.0 - double * sine, double * cosine


TOGETHER = 32


def render_kernel(near, basis, canvas, left, right, slots, tasks, slots_sem):
    sector = lax.axis_index("sector")
    slab = lax.axis_index("slab")
    base_row = 2 * LINES * slab + LINES * sector
    slots_copy = pltpu.make_async_copy(near.at[:, :, pl.ds(SLOTS, 8)], slots, slots_sem)
    slots_copy.start()
    canvas[...] = jnp.zeros_like(canvas)
    slots_copy.wait()

    def about(slot):
        hop = slot // (2 * SLOTS)
        side = slot // SLOTS % 2
        at = slot % SLOTS
        return [slots[hop, side, number, at] for number in range(4)]

    def collect(slot, counts):
        _, tile_row, _, live = about(slot)
        top = base_row - tile_row.astype(jnp.int32)
        found = []
        for part, count in enumerate(counts):
            start = top + part * HALF
            reaches = (start >= 17 - (HALF - 1)) & (start <= 238) & (live > 0.0)
            tasks[part, count] = slot
            found.append(count + reaches.astype(jnp.int32))
        return tuple(found)

    counts = lax.fori_loop(0, NEAR, collect, (0,) * (LINES // HALF))
    coeff = [
        jnp.concatenate([near[hop, side, :SLOTS, :MODES] for side in range(2)], axis=0).astype(BF16)
        for hop in range(3)
    ]
    for part in range(2):
        mix = jnp.concatenate([coeff[2 * part], coeff[1]], axis=0)

        @pl.loop(0, TILE // 2 // TOGETHER)
        def _(step):
            row = part * (TILE // 2) + step * TOGETHER
            columns = pl.ds(pl.multiple_of(row * TILE, TOGETHER * TILE), TOGETHER * TILE)
            phases = dot(mix, basis[:, columns])
            for extra in range(TOGETHER):
                place = pl.ds(pl.multiple_of((row + extra + PAD) * 64, 64), 64)
                at = extra * TILE
                left[place, :] = phases[:, at : at + 128]
                right[place, :] = phases[:, at + 128 : at + 256]

    lane = lax.broadcasted_iota(jnp.int32, (1, 128), 1)
    down = lax.broadcasted_iota(jnp.int32, (HALF, 1), 0)
    reach = 7 * (TILE - 2)

    def tile_part(slot, part, counted):
        reflectivity, tile_row, column, live = about(slot)
        weight = jnp.where(counted, reflectivity * live, 0.0)
        column = column.astype(jnp.int32)
        top = part * HALF + base_row - tile_row.astype(jnp.int32)
        block = column // 128
        shift = lax.rem(column, 128)
        start = (top + PAD) * 64 + lax.rem(slot, 64)
        vertical = jnp.abs(2 * (top + down) - (TILE - 1))
        vertical = jnp.where(8 * vertical <= reach, 4 * vertical, 4 * reach)
        vertical = jnp.broadcast_to(vertical, (HALF, 128))
        place = (lane - shift) & 127
        room_left = reach - 7 * ((TILE - 1) - 2 * place)
        room_right = reach - 7 * (2 * place + 1)
        both = []
        for ref, room in ((left, room_left), (right, room_right)):
            wave = pltpu.roll(ref[pl.ds(start, HALF, stride=64), :], shift, 1)
            inside = vertical <= room
            amplitude = jnp.where(inside, weight, 0.0)
            cosine, sine = circle(jnp.where(inside, wave, 0.0))
            both.append((cosine * amplitude, sine * amplitude))
        return block, jnp.broadcast_to(lane >= shift, (HALF, 128)), both

    for part in range(LINES // HALF):
        rows = pl.ds(part * HALF, HALF)
        count = counts[part]

        @pl.loop(0, (count + 1) // 2)
        def _(step):
            pieces = []
            for extra in range(2):
                at = 2 * step + extra
                pieces.append(tile_part(tasks[part, jnp.minimum(at, count - 1)], part, at < count))
            for block, kept, both in pieces:
                for comp in range(2):
                    one, two = both[0][comp], both[1][comp]
                    at = comp * BLOCKS + block
                    past = jnp.minimum(at + 2, 2 * BLOCKS - 1)
                    canvas[at, rows, :] += jnp.where(kept, one, 0.0)
                    canvas[at + 1, rows, :] += jnp.where(kept, two, one)
                    canvas[past, rows, :] += jnp.where(kept, 0.0, two)


def render(near, mode_basis):
    vmem = pl.BlockSpec(memory_space=pltpu.VMEM)
    return pl.pallas_call(
        render_kernel,
        out_shape=jax.ShapeDtypeStruct((2 * BLOCKS, LINES, 128), F32),
        in_specs=[vmem, vmem],
        out_specs=vmem,
        scratch_shapes=[
            pltpu.VMEM(((TILE + 2 * PAD) * 64, 128), F32),
            pltpu.VMEM(((TILE + 2 * PAD) * 64, 128), F32),
            pltpu.SMEM((3, 2, 8, 128), F32),
            pltpu.SMEM((LINES // HALF, NEAR), jnp.int32),
            pltpu.SemaphoreType.DMA,
        ],
        compiler_params=pltpu.CompilerParams(vmem_limit_bytes=40 << 20),
        name="render_rows",
    )(near, mode_basis)


def encode(value):
    size = jnp.log(jnp.abs(value)) * (STEPS / math.log(2.0)) + (LOW * STEPS + 0.5)
    code = jnp.maximum(size, 0.0).astype(jnp.int32)
    return jnp.where(value < 0.0, -code, code)


def decode(code):
    size = jnp.abs(code).astype(F32) * (math.log(2.0) / STEPS) - LOW * math.log(2.0)
    value = jnp.exp(size)
    return jnp.where(code == 0, 0.0, jnp.where(code < 0, -value, value))


def exchange_kernel(
    field, turn, twist, long_turn, mid_ref, wide, outbox, inbox, plain, send_sem, recv_sem
):
    sector = lax.axis_index("sector")
    slab = lax.axis_index("slab")
    me = sector * SLABS + slab
    source = 2 * slab + sector
    barrier = pltpu.get_barrier_semaphore()

    @pl.loop(1, DEVICES)
    def _(step):
        other = (me + step) & (DEVICES - 1)
        pl.semaphore_signal(
            barrier, inc=1, device_id=(other >> 6, other & (SLABS - 1)), device_id_type=MESH
        )

    lines = field.reshape(2 * BLOCKS * LINES, 128)
    codes = wide.reshape(DEVICES * CHUNK, 128)
    values = plain.reshape(DEVICES * CHUNK, 128)
    for chunk in range(CHUNKS):

        @pl.loop(0, CHUNK // 4)
        def _(step):
            parts = []
            for pair in range(2):
                line = chunk * CHUNK + 4 * step + 2 * pair
                both = [lines[pl.ds(line + e, 2 * BLOCKS, stride=LINES), :] for e in range(2)]
                mid = dot_short(turn[...], jnp.concatenate(both, axis=1))
                for e in range(2):
                    real = mid[:64, 128 * e : 128 * e + 128]
                    imag = mid[64:, 128 * e : 128 * e + 128]
                    turned_real = real * twist[0] + imag * twist[1]
                    turned_imag = imag * twist[0] - real * twist[1]
                    parts.append(jnp.concatenate([turned_real, turned_imag], axis=1))
            done = encode(dot_long(jnp.concatenate(parts, axis=0), long_turn))
            for e in range(4):
                some = done[64 * e : 64 * e + 64]
                some = jnp.concatenate([some[:, :128], some[:, 128:]], axis=0).T
                codes[pl.ds(4 * step + e, DEVICES, stride=CHUNK), :] = some

        @pl.loop(0, DEVICES // 16)
        def _(step):
            some = pl.ds(step * 16, 16)
            outbox[chunk, some] = wide[some].astype(jnp.int16)

        if chunk == 0:
            pl.semaphore_wait(barrier, DEVICES - 1)

        @pl.loop(1, DEVICES)
        def _(step):
            other = (me + step) & (DEVICES - 1)
            pltpu.make_async_remote_copy(
                src_ref=outbox.at[chunk, other],
                dst_ref=inbox.at[chunk, source],
                send_sem=send_sem.at[chunk],
                recv_sem=recv_sem.at[chunk],
                device_id=(other >> 6, other & (SLABS - 1)),
                device_id_type=MESH,
            ).start()

        inbox[chunk, source] = outbox[chunk, me]

    for chunk in range(CHUNKS):
        most = inbox.at[chunk, pl.ds(0, DEVICES - 1)]
        pltpu.make_async_copy(most, most, recv_sem.at[chunk]).wait()

        @pl.loop(0, DEVICES // 16)
        def _(step):
            some = pl.ds(step * 16, 16)
            plain[some] = decode(inbox[chunk, some].astype(jnp.int32))

        @pl.loop(0, CHUNK // 4)
        def _(step):
            parts = []
            for e in range(4):
                turned = values[pl.ds(4 * step + e, DEVICES, stride=CHUNK), :].T
                parts.append(jnp.concatenate([turned[:64], turned[64:]], axis=1))
            mid = dot_long(jnp.concatenate(parts, axis=0), long_turn)
            for e in range(4):
                line = chunk * CHUNK + 4 * step + e
                cos = twist[0, pl.ds(line, 1), :]
                sin = twist[1, pl.ds(line, 1), :]
                real = mid[64 * e : 64 * e + 64, :128]
                imag = mid[64 * e : 64 * e + 64, 128:]
                mid_ref[0, line] = real * cos + imag * sin
                mid_ref[1, line] = imag * cos - real * sin

    for chunk in range(CHUNKS):
        most = outbox.at[chunk, pl.ds(0, DEVICES - 1)]
        pltpu.make_async_copy(most, most, send_sem.at[chunk]).wait()


def exchange(field, *consts):
    vmem = pl.BlockSpec(memory_space=pltpu.VMEM)
    return pl.pallas_call(
        exchange_kernel,
        out_shape=jax.ShapeDtypeStruct((2, LINES, LINES, 128), F32),
        in_specs=[vmem] * 4,
        out_specs=vmem,
        scratch_shapes=[
            pltpu.VMEM((DEVICES, CHUNK, 128), jnp.int32),
            pltpu.VMEM((CHUNKS, DEVICES, CHUNK, 128), jnp.int16),
            pltpu.VMEM((CHUNKS, DEVICES, CHUNK, 128), jnp.int16),
            pltpu.VMEM((DEVICES, CHUNK, 128), F32),
            pltpu.SemaphoreType.DMA((CHUNKS,)),
            pltpu.SemaphoreType.DMA((CHUNKS,)),
        ],
        compiler_params=pltpu.CompilerParams(
            collective_id=1, has_side_effects=True, vmem_limit_bytes=32 << 20
        ),
        name="exchange",
    )(field, *consts)


def finish_kernel(mid_ref, turn, out_hbm, turned, ready, out_sem):
    lines = mid_ref.reshape(2 * LINES * LINES, 128)

    def leave(group):
        return pltpu.make_async_copy(
            ready.at[group % 2], out_hbm.at[:, pl.ds(group * 8, 8)], out_sem.at[group % 2]
        )

    for group in range(LINES // 8):
        for pair in range(4):
            line = group * 8 + 2 * pair
            both = [lines[pl.ds(line + e, 2 * LINES, stride=LINES), :] for e in range(2)]
            done = dot_short(turn[...], jnp.concatenate(both, axis=1))
            for e in range(2):
                turned[group % 2, pl.ds(2 * pair + e, 2 * LINES, stride=8), :] = done[
                    :, 128 * e : 128 * e + 128
                ]
        if group >= 2:
            leave(group - 2).wait()
        for comp in range(2):
            for block in range(LINES):
                at = (comp * LINES + block) * 8
                ready[group % 2, comp, :, 128 * block : 128 * block + 128] = turned[
                    group % 2, at : at + 8, :
                ]
        leave(group).start()
    for group in range(LINES // 8 - 2, LINES // 8):
        leave(group).wait()


def finish(mid, turn):
    vmem = pl.BlockSpec(memory_space=pltpu.VMEM)
    return pl.pallas_call(
        finish_kernel,
        out_shape=jax.ShapeDtypeStruct((2, LINES, GRID), F32),
        in_specs=[vmem, vmem],
        out_specs=pl.BlockSpec(memory_space=pl.ANY),
        scratch_shapes=[
            pltpu.VMEM((2, 2 * LINES * 8, 128), F32),
            pltpu.VMEM((2, 2, 8, GRID), F32),
            pltpu.SemaphoreType.DMA((2,)),
        ],
        compiler_params=pltpu.CompilerParams(vmem_limit_bytes=24 << 20),
        name="finish",
    )(mid, turn)


def body(mode_basis, mode_coeff, reflect, tile_row, tile_col, slot_live):
    turn, twist, long_turn, last_turn = (jnp.asarray(table) for table in tables())
    near, basis = gather_near(mode_basis, mode_coeff, reflect, tile_row, tile_col, slot_live)
    field = render(near, basis)
    mid = exchange(field, turn, twist, long_turn)
    return finish(mid, last_turn)


def solution(mesh):
    placed = (
        P(),
        P(("sector", "slab"), None),
        P(("sector", "slab")),
        P(("sector", "slab")),
        P(("sector", "slab")),
        P(("sector", "slab")),
    )
    return jax.shard_map(
        body,
        mesh=mesh,
        in_specs=placed,
        out_specs=P(None, ("sector", "slab"), None),
        check_vma=False,
    )
```

time: 72.5 us -> 65.9 us (0.909)
  Pallas kernels: 71.2 us -> 65.7 us
  local copies, waits for them, and re-layouts: 0.91 us -> 0.03 us
    pallas_call x1, Pallas kernels: 13.5 us -> 9.77 us  [render(): pl.pallas_call(render_kernel, out_shape=jax.ShapeDtypeStruct((2 * BLOCKS,...]
    pallas_call x1, Pallas kernels: 38.1 us -> 36.8 us  [exchange(): pl.pallas_call(exchange_kernel, out_shape=jax.ShapeDtypeStruct((2, LINES,...]
    unnamed x14 -> x8, local copies, waits for them, and re-layouts: 0.91 us -> 0.03 us
    pallas_call x1, Pallas kernels: 14.1 us -> 13.3 us  [gather_near(): pl.pallas_call(gather_kernel, out_shape=[jax.ShapeDtypeStruct((3, 2, SLOT...]
where the time goes in v3:
time: 65.9 us; the launch traced here: 65.8 us
  Pallas kernels  65.7 us (100%)
    pallas_call x1, Pallas kernels, exchange(): pl.pallas_call(exchange_kernel, out_shape=jax.ShapeDtypeStruct((2, LINES,...  36.8 us
    pallas_call x1, Pallas kernels, gather_near(): pl.pallas_call(gather_kernel, out_shape=[jax.ShapeDtypeStruct((3, 2, SLOT...  13.3 us
    pallas_call x1, Pallas kernels, render(): pl.pallas_call(render_kernel, out_shape=jax.ShapeDtypeStruct((2 * BLOCKS,...  9.77 us
    pallas_call x1, Pallas kernels, finish(): pl.pallas_call(finish_kernel, out_shape=jax.ShapeDtypeStruct((2, LINES, G...  5.78 us

profile of v3, /device:TPU:1, one launch (start us, length us, event | category | flops | bytes accessed | tf_op | source)
XLA Modules:
  0.0 65.8 jit_solution(16355933126146271869)
XLA Ops:
  0.0 13.3 %gather_near.1 = (f32[3,2,24,128]{3,2,1,0:T(8,128)S(1)}, bf16[64,65536]{1,0:T(8,128)(2,1)S(1)}) custom-call(bf16[64,65536]{1,0:T(8,128)(2,1)} %basis_hbm.1, bf16[16,64]{1,0:T(8,128)(2,1)} %coeff_hbm.1, bf16[1,16]{1,0:T(2,128)(2,1)} %bitcast.4, s32[1,16]{1,0:T(1,128)} %bitcast.5, s32[1,16]{1,0:T(1,128)} %bitcast.6, s32[1,16]{1,0:T(1,128)} %bitcast.7), custom_call_target="tpu_custom_call" | custom-call | tf_op jit(solution)/shard_map/gather_near/pallas_call | solution.py:163
  13.3 0.0 copy-start
  13.4 0.0 copy-start.2
  13.4 0.0 copy-start.3
  13.4 9.8 %render_rows.1.field = f32[128,64,128]{2,1,0:T(8,128)S(1)} custom-call(f32[3,2,24,128]{3,2,1,0:T(8,128)S(1)} %get-tuple-element.7.near, bf16[64,65536]{1,0:T(8,128)(2,1)S(1)} %get-tuple-element.8.basis), custom_call_target="tpu_custom_call" | custom-call | tf_op jit(solution)/shard_map/render_rows/pallas_call | solution.py:302
  23.2 0.0 copy-done
  23.2 0.0 copy-done.2
  23.2 0.0 copy-done.3
  23.2 0.0 copy-start.1
  23.2 36.8 %exchange.1.mid_ref = f32[2,64,64,128]{3,2,1,0:T(8,128)S(1)} custom-call(f32[128,64,128]{2,1,0:T(8,128)S(1)} %render_rows.1.field, bf16[256,256]{1,0:T(8,128)(2,1)S(1)} %copy-done.2, f32[2,64,128]{2,1,0:T(8,128)S(1)} %copy-done.3, bf16[2,256,256]{2,1,0:T(8,128)(2,1)S(1)} %copy-done), custom_call_target="tpu_custom_call" | custom-call | tf_op jit(solution)/shard_map/exchange/pallas_call | solution.py:425
  60.0 0.0 copy-done.1
  60.0 5.8 %finish.1 = f32[2,64,8192]{2,1,0:T(8,128)} custom-call(f32[2,64,64,128]{3,2,1,0:T(8,128)S(1)} %exchange.1.mid_ref, bf16[256,256]{1,0:T(8,128)(2,1)S(1)} %copy-done.1), custom_call_target="tpu_custom_call" | custom-call | tf_op jit(solution)/shard_map/finish/pallas_call | solution.py:477
Async XLA Ops:
  13.3 9.8 %copy-start = (bf16[2,256,256]{2,1,0:T(8,128)(2,1)S(1)}, bf16[2,256,256]{2,1,0:T(8,128)(2,1)}, u32[]{:S(2)}) copy-start(bf16[2,256,256]{2,1,0:T(8,128)(2,1)} %constant.10.clone.long_turn) | copy-start | bytes 786436
  13.4 9.8 %copy-start.2 = (bf16[256,256]{1,0:T(8,128)(2,1)S(1)}, bf16[256,256]{1,0:T(8,128)(2,1)}, u32[]{:S(2)}) copy-start(bf16[256,256]{1,0:T(8,128)(2,1)} %constant.8.clone.turn) | copy-start | bytes 393220
  13.4 9.8 %copy-start.3 = (f32[2,64,128]{2,1,0:T(8,128)S(1)}, f32[2,64,128]{2,1,0:T(8,128)}, u32[]{:S(2)}) copy-start(f32[2,64,128]{2,1,0:T(8,128)} %constant.9.clone.twist) | copy-start | bytes 196612
  23.2 36.8 %copy-start.1 = (bf16[256,256]{1,0:T(8,128)(2,1)S(1)}, bf16[256,256]{1,0:T(8,128)(2,1)}, u32[]{:S(2)}) copy-start(bf16[256,256]{1,0:T(8,128)(2,1)} %constant.11.clone.turn) | copy-start | bytes 393220

commit v4 on v3

--- a/solution.py
+++ b/solution.py
@@ -23,6 +23,9 @@
 CHUNKS = LINES // CHUNK
 PAD = 16
 HALF = 32
+FIRST, LAST = 16, 240
+WIDE = LINES + 8
+SHORT = CHUNK + 8
 MESH = pl.DeviceIdType.MESH
 F32 = jnp.float32
 BF16 = jnp.bfloat16
@@ -114,6 +117,8 @@
     sector = lax.axis_index("sector")
     slab = lax.axis_index("slab")
     barrier = pltpu.get_barrier_semaphore()
+    used = pl.ds(FIRST * TILE, (LAST - FIRST) * TILE)
+    basis_copy = pltpu.make_async_copy(basis_hbm.at[:, used], basis_ref, basis_sem)
     sources = (coeff_hbm, reflect_hbm, row_hbm, column_hbm, live_hbm)
     held = (coeff_ref, reflect_ref, row_ref, column_ref, live_ref)
     loads = [
@@ -122,6 +127,7 @@
     ]
     for load in loads:
         load.start()
+    basis_copy.start()
     others = [(flip, hop) for hop in range(3) for flip in range(2)][1:]
     for flip, hop in others:
         for step in {hop, -hop}:
@@ -131,8 +137,6 @@
                 device_id=(lax.rem(sector + flip, 2), lax.rem(slab + step + SLABS, SLABS)),
                 device_id_type=MESH,
             )
-    basis_copy = pltpu.make_async_copy(basis_hbm, basis_ref, basis_sem)
-    basis_copy.start()
     for load in loads:
         load.wait()
     own[:SLOTS, :MODES] = coeff_ref[...].astype(F32)
@@ -164,7 +168,7 @@
         gather_kernel,
         out_shape=[
             jax.ShapeDtypeStruct((3, 2, SLOTS + 8, 128), F32),
-            jax.ShapeDtypeStruct(mode_basis.shape, BF16),
+            jax.ShapeDtypeStruct((MODES, (LAST - FIRST) * TILE), BF16),
         ],
         in_specs=[pl.BlockSpec(memory_space=pltpu.HBM)] * 6,
         out_specs=[vmem, vmem],
@@ -202,66 +206,86 @@
     return 1.0 - double * sine, double * cosine
 
 
-TOGETHER = 32
-
-
-def render_kernel(near, basis, canvas, left, right, slots, tasks, slots_sem):
+TOGETHER = 28
+STEPS_EACH = (LAST - FIRST) // 2 // TOGETHER
+LISTED = NEAR // STEPS_EACH
+TASKS = 4
+
+
+def render_kernel(
+    near, basis, canvas, left, right, marks, slots, table, tasks, slots_sem, table_sem
+):
     sector = lax.axis_index("sector")
     slab = lax.axis_index("slab")
     base_row = 2 * LINES * slab + LINES * sector
     slots_copy = pltpu.make_async_copy(near.at[:, :, pl.ds(SLOTS, 8)], slots, slots_sem)
     slots_copy.start()
+    for hop in range(3):
+        for side in range(2):
+            tile_row, column, live = (
+                near[hop, side, SLOTS + number : SLOTS + number + 1, :].astype(jnp.int32)
+                for number in (1, 2, 3)
+            )
+            top = base_row - tile_row
+            at = 2 * hop + side
+            marks[at, 0:1, :] = top
+            marks[at, 1:2, :] = column >> 7
+            marks[at, 2:3, :] = column & 127
+            for part in range(2):
+                start = top + part * HALF
+                reaches = (start >= 17 - (HALF - 1)) & (start <= 238) & (live > 0)
+                marks[at, 3 + part : 4 + part, :] = reaches.astype(jnp.int32)
+    table_copy = pltpu.make_async_copy(marks, table, table_sem)
+    table_copy.start()
     canvas[...] = jnp.zeros_like(canvas)
-    slots_copy.wait()
-
-    def about(slot):
-        hop = slot // (2 * SLOTS)
-        side = slot // SLOTS % 2
-        at = slot % SLOTS
-        return [slots[hop, side, number, at] for number in range(4)]
-
-    def collect(slot, counts):
-        _, tile_row, _, live = about(slot)
-        top = base_row - tile_row.astype(jnp.int32)
-        found = []
-        for part, count in enumerate(counts):
-            start = top + part * HALF
-            reaches = (start >= 17 - (HALF - 1)) & (start <= 238) & (live > 0.0)
-            tasks[part, count] = slot
-            found.append(count + reaches.astype(jnp.int32))
-        return tuple(found)
-
-    counts = lax.fori_loop(0, NEAR, collect, (0,) * (LINES // HALF))
     coeff = [
         jnp.concatenate([near[hop, side, :SLOTS, :MODES] for side in range(2)], axis=0).astype(BF16)
         for hop in range(3)
     ]
-    for part in range(2):
+
+    def form(part, step):
         mix = jnp.concatenate([coeff[2 * part], coeff[1]], axis=0)
-
-        @pl.loop(0, TILE // 2 // TOGETHER)
-        def _(step):
-            row = part * (TILE // 2) + step * TOGETHER
-            columns = pl.ds(pl.multiple_of(row * TILE, TOGETHER * TILE), TOGETHER * TILE)
-            phases = dot(mix, basis[:, columns])
-            for extra in range(TOGETHER):
-                place = pl.ds(pl.multiple_of((row + extra + PAD) * 64, 64), 64)
-                at = extra * TILE
-                left[place, :] = phases[:, at : at + 128]
-                right[place, :] = phases[:, at + 128 : at + 256]
-
+        row = (part * STEPS_EACH + step) * TOGETHER
+        columns = pl.ds(pl.multiple_of(row * TILE, TOGETHER * TILE), TOGETHER * TILE)
+        phases = dot(mix, basis[:, columns])
+        for extra in range(TOGETHER):
+            place = pl.ds(pl.multiple_of((row + extra + FIRST + PAD) * WIDE, 8), 64)
+            at = extra * TILE
+            left[place, :] = phases[:, at : at + 128]
+            right[place, :] = phases[:, at + 128 : at + 256]
+
+    @pl.loop(0, STEPS_EACH)
+    def _(step):
+        form(0, step)
+
+    table_copy.wait()
+    slots_copy.wait()
+
+    def form_and_list(step, count):
+        form(1, step)
+        for extra in range(LISTED):
+            slot = step * LISTED + extra
+            for part in range(2):
+                tasks[count] = 2 * slot + part
+                count = count + table[slot >> 4, 3 + part, slot & 15]
+        return count
+
+    count = lax.fori_loop(0, STEPS_EACH, form_and_list, 0)
     lane = lax.broadcasted_iota(jnp.int32, (1, 128), 1)
     down = lax.broadcasted_iota(jnp.int32, (HALF, 1), 0)
     reach = 7 * (TILE - 2)
 
-    def tile_part(slot, part, counted):
-        reflectivity, tile_row, column, live = about(slot)
-        weight = jnp.where(counted, reflectivity * live, 0.0)
-        column = column.astype(jnp.int32)
-        top = part * HALF + base_row - tile_row.astype(jnp.int32)
-        block = column // 128
-        shift = lax.rem(column, 128)
-        start = (top + PAD) * 64 + lax.rem(slot, 64)
+    def tile_part(number):
+        task = tasks[jnp.minimum(number, count - 1)]
+        slot = task >> 1
+        part = task & 1
+        group = slot >> 4
+        at = slot & 15
+        weight = jnp.where(number < count, slots[slot >> 5, group & 1, 0, at], 0.0)
+        top = table[group, 0, at] + part * HALF
+        block = table[group, 1, at]
+        shift = table[group, 2, at]
+        start = (top + PAD) * WIDE + (slot & 63)
         vertical = jnp.abs(2 * (top + down) - (TILE - 1))
         vertical = jnp.where(8 * vertical <= reach, 4 * vertical, 4 * reach)
         vertical = jnp.broadcast_to(vertical, (HALF, 128))
@@ -270,45 +294,49 @@
         room_right = reach - 7 * (2 * place + 1)
         both = []
         for ref, room in ((left, room_left), (right, room_right)):
-            wave = pltpu.roll(ref[pl.ds(start, HALF, stride=64), :], shift, 1)
+            wave = pltpu.roll(ref[pl.ds(start, HALF, stride=WIDE), :], shift, 1)
             inside = vertical <= room
             amplitude = jnp.where(inside, weight, 0.0)
             cosine, sine = circle(jnp.where(inside, wave, 0.0))
             both.append((cosine * amplitude, sine * amplitude))
-        return block, jnp.broadcast_to(lane >= shift, (HALF, 128)), both
-
-    for part in range(LINES // HALF):
-        rows = pl.ds(part * HALF, HALF)
-        count = counts[part]
-
-        @pl.loop(0, (count + 1) // 2)
-        def _(step):
-            pieces = []
-            for extra in range(2):
-                at = 2 * step + extra
-                pieces.append(tile_part(tasks[part, jnp.minimum(at, count - 1)], part, at < count))
-            for block, kept, both in pieces:
-                for comp in range(2):
-                    one, two = both[0][comp], both[1][comp]
-                    at = comp * BLOCKS + block
-                    past = jnp.minimum(at + 2, 2 * BLOCKS - 1)
-                    canvas[at, rows, :] += jnp.where(kept, one, 0.0)
-                    canvas[at + 1, rows, :] += jnp.where(kept, two, one)
-                    canvas[past, rows, :] += jnp.where(kept, 0.0, two)
+        rows = pl.ds(pl.multiple_of(part * HALF, HALF), HALF)
+        return block, rows, jnp.broadcast_to(lane >= shift, (HALF, 128)), both
+
+    def deposit(block, rows, kept, both):
+        for comp in range(2):
+            one, two = both[0][comp], both[1][comp]
+            at = comp * BLOCKS + block
+            past = jnp.minimum(at + 2, 2 * BLOCKS - 1)
+            canvas[at, rows, :] += jnp.where(kept, one, 0.0)
+            canvas[at + 1, rows, :] += jnp.where(kept, two, one)
+            canvas[past, rows, :] += jnp.where(kept, 0.0, two)
+
+    @pl.loop(0, (count + TASKS - 1) // TASKS)
+    def _(step):
+        before = None
+        for extra in range(TASKS):
+            piece = tile_part(TASKS * step + extra)
+            if before is not None:
+                deposit(*before)
+            before = piece
+        deposit(*before)
 
 
 def render(near, mode_basis):
     vmem = pl.BlockSpec(memory_space=pltpu.VMEM)
     return pl.pallas_call(
         render_kernel,
-        out_shape=jax.ShapeDtypeStruct((2 * BLOCKS, LINES, 128), F32),
+        out_shape=jax.ShapeDtypeStruct((2 * BLOCKS, WIDE, 128), F32),
         in_specs=[vmem, vmem],
         out_specs=vmem,
         scratch_shapes=[
-            pltpu.VMEM(((TILE + 2 * PAD) * 64, 128), F32),
-            pltpu.VMEM(((TILE + 2 * PAD) * 64, 128), F32),
+            pltpu.VMEM(((TILE + 2 * PAD) * WIDE, 128), F32),
+            pltpu.VMEM(((TILE + 2 * PAD) * WIDE, 128), F32),
+            pltpu.VMEM((6, 8, 128), jnp.int32),
             pltpu.SMEM((3, 2, 8, 128), F32),
-            pltpu.SMEM((LINES // HALF, NEAR), jnp.int32),
+            pltpu.SMEM((6, 8, 128), jnp.int32),
+            pltpu.SMEM((2 * NEAR + 8,), jnp.int32),
+            pltpu.SemaphoreType.DMA,
             pltpu.SemaphoreType.DMA,
         ],
         compiler_params=pltpu.CompilerParams(vmem_limit_bytes=40 << 20),
@@ -344,9 +372,9 @@
             barrier, inc=1, device_id=(other >> 6, other & (SLABS - 1)), device_id_type=MESH
         )
 
-    lines = field.reshape(2 * BLOCKS * LINES, 128)
-    codes = wide.reshape(DEVICES * CHUNK, 128)
-    values = plain.reshape(DEVICES * CHUNK, 128)
+    lines = field.reshape(2 * BLOCKS * WIDE, 128)
+    codes = wide.reshape(DEVICES * SHORT, 128)
+    values = plain.reshape(DEVICES * SHORT, 128)
     for chunk in range(CHUNKS):
 
         @pl.loop(0, CHUNK // 4)
@@ -354,7 +382,7 @@
             parts = []
             for pair in range(2):
                 line = chunk * CHUNK + 4 * step + 2 * pair
-                both = [lines[pl.ds(line + e, 2 * BLOCKS, stride=LINES), :] for e in range(2)]
+                both = [lines[pl.ds(line + e, 2 * BLOCKS, stride=WIDE), :] for e in range(2)]
                 mid = dot_short(turn[...], jnp.concatenate(both, axis=1))
                 for e in range(2):
                     real = mid[:64, 128 * e : 128 * e + 128]
@@ -366,12 +394,12 @@
             for e in range(4):
                 some = done[64 * e : 64 * e + 64]
                 some = jnp.concatenate([some[:, :128], some[:, 128:]], axis=0).T
-                codes[pl.ds(4 * step + e, DEVICES, stride=CHUNK), :] = some
+                codes[pl.ds(4 * step + e, DEVICES, stride=SHORT), :] = some
 
         @pl.loop(0, DEVICES // 16)
         def _(step):
             some = pl.ds(step * 16, 16)
-            outbox[chunk, some] = wide[some].astype(jnp.int16)
+            outbox[chunk, some] = wide[some, :CHUNK].astype(jnp.int16)
 
         if chunk == 0:
             pl.semaphore_wait(barrier, DEVICES - 1)
@@ -397,13 +425,13 @@
         @pl.loop(0, DEVICES // 16)
         def _(step):
             some = pl.ds(step * 16, 16)
-            plain[some] = decode(inbox[chunk, some].astype(jnp.int32))
+            plain[some, :CHUNK] = decode(inbox[chunk, some].astype(jnp.int32))
 
         @pl.loop(0, CHUNK // 4)
         def _(step):
             parts = []
             for e in range(4):
-                turned = values[pl.ds(4 * step + e, DEVICES, stride=CHUNK), :].T
+                turned = values[pl.ds(4 * step + e, DEVICES, stride=SHORT), :].T
                 parts.append(jnp.concatenate([turned[:64], turned[64:]], axis=1))
             mid = dot_long(jnp.concatenate(parts, axis=0), long_turn)
             for e in range(4):
@@ -412,8 +440,8 @@
                 sin = twist[1, pl.ds(line, 1), :]
                 real = mid[64 * e : 64 * e + 64, :128]
                 imag = mid[64 * e : 64 * e + 64, 128:]
-                mid_ref[0, line] = real * cos + imag * sin
-                mid_ref[1, line] = imag * cos - real * sin
+                mid_ref[0, line, :LINES] = real * cos + imag * sin
+                mid_ref[1, line, :LINES] = imag * cos - real * sin
 
     for chunk in range(CHUNKS):
         most = outbox.at[chunk, pl.ds(0, DEVICES - 1)]
@@ -424,14 +452,14 @@
     vmem = pl.BlockSpec(memory_space=pltpu.VMEM)
     return pl.pallas_call(
         exchange_kernel,
-        out_shape=jax.ShapeDtypeStruct((2, LINES, LINES, 128), F32),
+        out_shape=jax.ShapeDtypeStruct((2, LINES, WIDE, 128), F32),
         in_specs=[vmem] * 4,
         out_specs=vmem,
         scratch_shapes=[
-            pltpu.VMEM((DEVICES, CHUNK, 128), jnp.int32),
+            pltpu.VMEM((DEVICES, SHORT, 128), jnp.int32),
             pltpu.VMEM((CHUNKS, DEVICES, CHUNK, 128), jnp.int16),
             pltpu.VMEM((CHUNKS, DEVICES, CHUNK, 128), jnp.int16),
-            pltpu.VMEM((DEVICES, CHUNK, 128), F32),
+            pltpu.VMEM((DEVICES, SHORT, 128), F32),
             pltpu.SemaphoreType.DMA((CHUNKS,)),
             pltpu.SemaphoreType.DMA((CHUNKS,)),
         ],
@@ -443,32 +471,29 @@
 
 
 def finish_kernel(mid_ref, turn, out_hbm, turned, ready, out_sem):
-    lines = mid_ref.reshape(2 * LINES * LINES, 128)
+    lines = mid_ref.reshape(2 * LINES * WIDE, 128)
 
     def leave(group):
-        return pltpu.make_async_copy(
-            ready.at[group % 2], out_hbm.at[:, pl.ds(group * 8, 8)], out_sem.at[group % 2]
-        )
+        rows = pl.ds(group * 8, 8)
+        return pltpu.make_async_copy(ready.at[:, rows], out_hbm.at[:, rows], out_sem.at[group])
 
     for group in range(LINES // 8):
         for pair in range(4):
             line = group * 8 + 2 * pair
-            both = [lines[pl.ds(line + e, 2 * LINES, stride=LINES), :] for e in range(2)]
+            both = [lines[pl.ds(line + e, 2 * LINES, stride=WIDE), :] for e in range(2)]
             done = dot_short(turn[...], jnp.concatenate(both, axis=1))
             for e in range(2):
                 turned[group % 2, pl.ds(2 * pair + e, 2 * LINES, stride=8), :] = done[
                     :, 128 * e : 128 * e + 128
                 ]
-        if group >= 2:
-            leave(group - 2).wait()
         for comp in range(2):
             for block in range(LINES):
                 at = (comp * LINES + block) * 8
-                ready[group % 2, comp, :, 128 * block : 128 * block + 128] = turned[
+                ready[comp, 8 * group : 8 * group + 8, 128 * block : 128 * block + 128] = turned[
                     group % 2, at : at + 8, :
                 ]
         leave(group).start()
-    for group in range(LINES // 8 - 2, LINES // 8):
+    for group in range(LINES // 8):
         leave(group).wait()
 
 
@@ -481,8 +506,8 @@
         out_specs=pl.BlockSpec(memory_space=pl.ANY),
         scratch_shapes=[
             pltpu.VMEM((2, 2 * LINES * 8, 128), F32),
-            pltpu.VMEM((2, 2, 8, GRID), F32),
-            pltpu.SemaphoreType.DMA((2,)),
+            pltpu.VMEM((2, LINES, GRID), F32),
+            pltpu.SemaphoreType.DMA((LINES // 8,)),
         ],
         compiler_params=pltpu.CompilerParams(vmem_limit_bytes=24 << 20),
         name="finish",

time: 65.9 us -> 55.9 us (0.85)
  Pallas kernels: 65.7 us -> 55.5 us
    pallas_call x1, Pallas kernels: 9.77 us -> 4.89 us  [render(): pl.pallas_call(render_kernel, out_shape=jax.ShapeDtypeStruct((2 * BLOCKS,...]
    pallas_call x1, Pallas kernels: 5.78 us -> 2.85 us  [finish(): pl.pallas_call(finish_kernel, out_shape=jax.ShapeDtypeStruct((2, LINES, G...]
    pallas_call x1, Pallas kernels: 36.8 us -> 34.4 us  [exchange(): pl.pallas_call(exchange_kernel, out_shape=jax.ShapeDtypeStruct((2, LINES,...]
where the time goes in v4:
time: 55.9 us; the launch traced here: 55.6 us
  Pallas kernels  55.5 us (99%)
    pallas_call x1, Pallas kernels, exchange(): pl.pallas_call(exchange_kernel, out_shape=jax.ShapeDtypeStruct((2, LINES,...  34.4 us
    pallas_call x1, Pallas kernels, gather_near(): pl.pallas_call(gather_kernel, out_shape=[jax.ShapeDtypeStruct((3, 2, SLOT...  13.3 us
    pallas_call x1, Pallas kernels, render(): pl.pallas_call(render_kernel, out_shape=jax.ShapeDtypeStruct((2 * BLOCKS,...  4.89 us
    pallas_call x1, Pallas kernels, finish(): pl.pallas_call(finish_kernel, out_shape=jax.ShapeDtypeStruct((2, LINES, G...  2.85 us

profile of v4, /device:TPU:1, one launch (start us, length us, event | category | flops | bytes accessed | tf_op | source)
XLA Modules:
  0.0 55.6 jit_solution(7145151203218472910)
XLA Ops:
  0.0 13.3 %gather_near.1 = (f32[3,2,24,128]{3,2,1,0:T(8,128)S(1)}, bf16[64,57344]{1,0:T(8,128)(2,1)S(1)}) custom-call(bf16[64,65536]{1,0:T(8,128)(2,1)} %basis_hbm.1, bf16[16,64]{1,0:T(8,128)(2,1)} %coeff_hbm.1, bf16[1,16]{1,0:T(2,128)(2,1)} %bitcast.4, s32[1,16]{1,0:T(1,128)} %bitcast.5, s32[1,16]{1,0:T(1,128)} %bitcast.6, s32[1,16]{1,0:T(1,128)} %bitcast.7), custom_call_target="tpu_custom_call" | custom-call | tf_op jit(solution)/shard_map/gather_near/pallas_call | solution.py:167
  13.3 0.0 copy-start
  13.4 0.0 copy-start.2
  13.4 0.0 copy-start.3
  13.4 4.9 %render_rows.1.field = f32[128,72,128]{2,1,0:T(8,128)S(1)} custom-call(f32[3,2,24,128]{3,2,1,0:T(8,128)S(1)} %get-tuple-element.7.near, bf16[64,57344]{1,0:T(8,128)(2,1)S(1)} %get-tuple-element.8.basis), custom_call_target="tpu_custom_call" | custom-call | tf_op jit(solution)/shard_map/render_rows/pallas_call | solution.py:327
  18.3 0.0 copy-done
  18.3 0.0 copy-done.2
  18.3 0.0 copy-done.3
  18.3 0.0 copy-start.1
  18.3 34.4 %exchange.1.mid_ref = f32[2,64,72,128]{3,2,1,0:T(8,128)S(1)} custom-call(f32[128,72,128]{2,1,0:T(8,128)S(1)} %render_rows.1.field, bf16[256,256]{1,0:T(8,128)(2,1)S(1)} %copy-done.2, f32[2,64,128]{2,1,0:T(8,128)S(1)} %copy-done.3, bf16[2,256,256]{2,1,0:T(8,128)(2,1)S(1)} %copy-done), custom_call_target="tpu_custom_call" | custom-call | tf_op jit(solution)/shard_map/exchange/pallas_call | solution.py:453
  52.8 0.0 copy-done.1
  52.8 2.9 %finish.1 = f32[2,64,8192]{2,1,0:T(8,128)} custom-call(f32[2,64,72,128]{3,2,1,0:T(8,128)S(1)} %exchange.1.mid_ref, bf16[256,256]{1,0:T(8,128)(2,1)S(1)} %copy-done.1), custom_call_target="tpu_custom_call" | custom-call | tf_op jit(solution)/shard_map/finish/pallas_call | solution.py:502
Async XLA Ops:
  13.3 4.9 %copy-start = (bf16[2,256,256]{2,1,0:T(8,128)(2,1)S(1)}, bf16[2,256,256]{2,1,0:T(8,128)(2,1)}, u32[]{:S(2)}) copy-start(bf16[2,256,256]{2,1,0:T(8,128)(2,1)} %constant.10.clone.long_turn) | copy-start | bytes 786436
  13.4 4.9 %copy-start.2 = (bf16[256,256]{1,0:T(8,128)(2,1)S(1)}, bf16[256,256]{1,0:T(8,128)(2,1)}, u32[]{:S(2)}) copy-start(bf16[256,256]{1,0:T(8,128)(2,1)} %constant.8.clone.turn) | copy-start | bytes 393220
  13.4 4.9 %copy-start.3 = (f32[2,64,128]{2,1,0:T(8,128)S(1)}, f32[2,64,128]{2,1,0:T(8,128)}, u32[]{:S(2)}) copy-start(f32[2,64,128]{2,1,0:T(8,128)} %constant.9.clone.twist) | copy-start | bytes 196612
  18.3 34.5 %copy-start.1 = (bf16[256,256]{1,0:T(8,128)(2,1)S(1)}, bf16[256,256]{1,0:T(8,128)(2,1)}, u32[]{:S(2)}) copy-start(bf16[256,256]{1,0:T(8,128)(2,1)} %constant.11.clone.turn) | copy-start | bytes 393220

commit v5 on v4

--- a/solution.py
+++ b/solution.py
@@ -357,19 +357,44 @@
 
 
 def exchange_kernel(
-    field, turn, twist, long_turn, mid_ref, wide, outbox, inbox, plain, send_sem, recv_sem
+    field,
+    turn,
+    twist,
+    long_turn,
+    mid_ref,
+    wide,
+    box,
+    handed,
+    early,
+    inbox,
+    plain,
+    send_sem,
+    recv_sem,
+    swap_send_sem,
+    swap_recv_sem,
 ):
     sector = lax.axis_index("sector")
     slab = lax.axis_index("slab")
-    me = sector * SLABS + slab
-    source = 2 * slab + sector
+    other_sector = 1 - sector
     barrier = pltpu.get_barrier_semaphore()
 
-    @pl.loop(1, DEVICES)
+    def greet(target):
+        pl.semaphore_signal(barrier, inc=1, device_id=target, device_id_type=MESH)
+
+    greet((other_sector, slab))
+
+    @pl.loop(1, SLABS, unroll=9)
     def _(step):
-        other = (me + step) & (DEVICES - 1)
-        pl.semaphore_signal(
-            barrier, inc=1, device_id=(other >> 6, other & (SLABS - 1)), device_id_type=MESH
+        greet((sector, (slab + step) & (SLABS - 1)))
+
+    def swap(chunk):
+        return pltpu.make_async_remote_copy(
+            src_ref=early.at[:, other_sector] if chunk == 0 else handed.at[chunk - 1],
+            dst_ref=(inbox if chunk == 0 else box).at[chunk, :, sector],
+            send_sem=swap_send_sem.at[chunk],
+            recv_sem=swap_recv_sem.at[chunk],
+            device_id=(other_sector, slab),
+            device_id_type=MESH,
         )
 
     lines = field.reshape(2 * BLOCKS * WIDE, 128)
@@ -396,36 +421,49 @@
                 some = jnp.concatenate([some[:, :128], some[:, 128:]], axis=0).T
                 codes[pl.ds(4 * step + e, DEVICES, stride=SHORT), :] = some
 
+        @pl.loop(0, SLABS // 16)
+        def _(step):
+            some = pl.ds(step * 16, 16)
+            for side, to in ((sector, sector), (other_sector, other_sector)):
+                packed = wide[pl.ds(to * SLABS + step * 16, 16), :CHUNK].astype(jnp.int16)
+                if chunk > 0 and side is other_sector:
+                    handed[chunk - 1, some] = packed
+                else:
+                    box[chunk, some, side] = packed
+
+        if chunk == 0:
+            pl.semaphore_wait(barrier, SLABS)
+        else:
+            swap(chunk).start()
+            swap(chunk).wait()
+        land = early if chunk == 0 else inbox.at[chunk]
+
+        @pl.loop(1, SLABS, unroll=3)
+        def _(step):
+            target = (slab + step) & (SLABS - 1)
+            pltpu.make_async_remote_copy(
+                src_ref=box.at[chunk, target],
+                dst_ref=land.at[slab],
+                send_sem=send_sem.at[chunk],
+                recv_sem=recv_sem.at[chunk],
+                device_id=(sector, target),
+                device_id_type=MESH,
+            ).start()
+
+        land[slab] = box[chunk, slab]
+
+    for chunk in range(CHUNKS):
+        most = (early if chunk == 0 else inbox.at[chunk]).at[pl.ds(0, SLABS - 1)]
+        pltpu.make_async_copy(most, most, recv_sem.at[chunk]).wait()
+        if chunk == 0:
+            swap(0).start()
+            inbox[0, :, sector] = early[:, sector]
+            swap(0).wait()
+
         @pl.loop(0, DEVICES // 16)
         def _(step):
-            some = pl.ds(step * 16, 16)
-            outbox[chunk, some] = wide[some, :CHUNK].astype(jnp.int16)
-
-        if chunk == 0:
-            pl.semaphore_wait(barrier, DEVICES - 1)
-
-        @pl.loop(1, DEVICES)
-        def _(step):
-            other = (me + step) & (DEVICES - 1)
-            pltpu.make_async_remote_copy(
-                src_ref=outbox.at[chunk, other],
-                dst_ref=inbox.at[chunk, source],
-                send_sem=send_sem.at[chunk],
-                recv_sem=recv_sem.at[chunk],
-                device_id=(other >> 6, other & (SLABS - 1)),
-                device_id_type=MESH,
-            ).start()
-
-        inbox[chunk, source] = outbox[chunk, me]
-
-    for chunk in range(CHUNKS):
-        most = inbox.at[chunk, pl.ds(0, DEVICES - 1)]
-        pltpu.make_async_copy(most, most, recv_sem.at[chunk]).wait()
-
-        @pl.loop(0, DEVICES // 16)
-        def _(step):
-            some = pl.ds(step * 16, 16)
-            plain[some, :CHUNK] = decode(inbox[chunk, some].astype(jnp.int32))
+            codes_in = inbox[chunk, pl.ds(step * 8, 8)].astype(jnp.int32)
+            plain[pl.ds(step * 16, 16), :CHUNK] = decode(codes_in).reshape(16, CHUNK, 128)
 
         @pl.loop(0, CHUNK // 4)
         def _(step):
@@ -444,7 +482,7 @@
                 mid_ref[1, line, :LINES] = imag * cos - real * sin
 
     for chunk in range(CHUNKS):
-        most = outbox.at[chunk, pl.ds(0, DEVICES - 1)]
+        most = box.at[chunk, pl.ds(0, SLABS - 1)]
         pltpu.make_async_copy(most, most, send_sem.at[chunk]).wait()
 
 
@@ -457,9 +495,13 @@
         out_specs=vmem,
         scratch_shapes=[
             pltpu.VMEM((DEVICES, SHORT, 128), jnp.int32),
-            pltpu.VMEM((CHUNKS, DEVICES, CHUNK, 128), jnp.int16),
-            pltpu.VMEM((CHUNKS, DEVICES, CHUNK, 128), jnp.int16),
+            pltpu.VMEM((CHUNKS, SLABS, 2, CHUNK, 128), jnp.int16),
+            pltpu.VMEM((CHUNKS - 1, SLABS, CHUNK, 128), jnp.int16),
+            pltpu.VMEM((SLABS, 2, CHUNK, 128), jnp.int16),
+            pltpu.VMEM((CHUNKS, SLABS, 2, CHUNK, 128), jnp.int16),
             pltpu.VMEM((DEVICES, SHORT, 128), F32),
+            pltpu.SemaphoreType.DMA((CHUNKS,)),
+            pltpu.SemaphoreType.DMA((CHUNKS,)),
             pltpu.SemaphoreType.DMA((CHUNKS,)),
             pltpu.SemaphoreType.DMA((CHUNKS,)),
         ],

time: 55.9 us -> 54.3 us (0.971)
  Pallas kernels: 55.5 us -> 54.1 us
    pallas_call x1, Pallas kernels: 34.4 us -> 33.5 us  [exchange(): pl.pallas_call(exchange_kernel, out_shape=jax.ShapeDtypeStruct((2, LINES,...]
where the time goes in v5:
time: 54.3 us; the launch traced here: 54.2 us
  Pallas kernels  54.1 us (100%)
    pallas_call x1, Pallas kernels, exchange(): pl.pallas_call(exchange_kernel, out_shape=jax.ShapeDtypeStruct((2, LINES,...  33.5 us
    pallas_call x1, Pallas kernels, gather_near(): pl.pallas_call(gather_kernel, out_shape=[jax.ShapeDtypeStruct((3, 2, SLOT...  13.3 us
    pallas_call x1, Pallas kernels, render(): pl.pallas_call(render_kernel, out_shape=jax.ShapeDtypeStruct((2 * BLOCKS,...  4.41 us
    pallas_call x1, Pallas kernels, finish(): pl.pallas_call(finish_kernel, out_shape=jax.ShapeDtypeStruct((2, LINES, G...  2.85 us

profile of v5, /device:TPU:1, one launch (start us, length us, event | category | flops | bytes accessed | tf_op | source)
XLA Modules:
  0.0 54.2 jit_solution(13847241434610134067)
XLA Ops:
  0.0 13.3 %gather_near.1 = (f32[3,2,24,128]{3,2,1,0:T(8,128)S(1)}, bf16[64,57344]{1,0:T(8,128)(2,1)S(1)}) custom-call(bf16[64,65536]{1,0:T(8,128)(2,1)} %basis_hbm.1, bf16[16,64]{1,0:T(8,128)(2,1)} %coeff_hbm.1, bf16[1,16]{1,0:T(2,128)(2,1)} %bitcast.4, s32[1,16]{1,0:T(1,128)} %bitcast.5, s32[1,16]{1,0:T(1,128)} %bitcast.6, s32[1,16]{1,0:T(1,128)} %bitcast.7), custom_call_target="tpu_custom_call" | custom-call | tf_op jit(solution)/shard_map/gather_near/pallas_call | solution.py:167
  13.3 0.0 copy-start
  13.4 0.0 copy-start.2
  13.4 0.0 copy-start.3
  13.4 4.4 %render_rows.1.field = f32[128,72,128]{2,1,0:T(8,128)S(1)} custom-call(f32[3,2,24,128]{3,2,1,0:T(8,128)S(1)} %get-tuple-element.7.near, bf16[64,57344]{1,0:T(8,128)(2,1)S(1)} %get-tuple-element.8.basis), custom_call_target="tpu_custom_call" | custom-call | tf_op jit(solution)/shard_map/render_rows/pallas_call | solution.py:327
  17.8 0.0 copy-done
  17.8 0.0 copy-done.2
  17.8 0.0 copy-done.3
  17.8 0.0 copy-start.1
  17.8 33.5 %exchange.1.mid_ref = f32[2,64,72,128]{3,2,1,0:T(8,128)S(1)} custom-call(f32[128,72,128]{2,1,0:T(8,128)S(1)} %render_rows.1.field, bf16[256,256]{1,0:T(8,128)(2,1)S(1)} %copy-done.2, f32[2,64,128]{2,1,0:T(8,128)S(1)} %copy-done.3, bf16[2,256,256]{2,1,0:T(8,128)(2,1)S(1)} %copy-done), custom_call_target="tpu_custom_call" | custom-call | tf_op jit(solution)/shard_map/exchange/pallas_call | solution.py:491
  51.4 0.0 copy-done.1
  51.4 2.9 %finish.1 = f32[2,64,8192]{2,1,0:T(8,128)} custom-call(f32[2,64,72,128]{3,2,1,0:T(8,128)S(1)} %exchange.1.mid_ref, bf16[256,256]{1,0:T(8,128)(2,1)S(1)} %copy-done.1), custom_call_target="tpu_custom_call" | custom-call | tf_op jit(solution)/shard_map/finish/pallas_call | solution.py:544
Async XLA Ops:
  13.3 4.5 %copy-start = (bf16[2,256,256]{2,1,0:T(8,128)(2,1)S(1)}, bf16[2,256,256]{2,1,0:T(8,128)(2,1)}, u32[]{:S(2)}) copy-start(bf16[2,256,256]{2,1,0:T(8,128)(2,1)} %constant.10.clone.long_turn) | copy-start | bytes 786436
  13.4 4.5 %copy-start.2 = (bf16[256,256]{1,0:T(8,128)(2,1)S(1)}, bf16[256,256]{1,0:T(8,128)(2,1)}, u32[]{:S(2)}) copy-start(bf16[256,256]{1,0:T(8,128)(2,1)} %constant.8.clone.turn) | copy-start | bytes 393220
  13.4 4.5 %copy-start.3 = (f32[2,64,128]{2,1,0:T(8,128)S(1)}, f32[2,64,128]{2,1,0:T(8,128)}, u32[]{:S(2)}) copy-start(f32[2,64,128]{2,1,0:T(8,128)} %constant.9.clone.twist) | copy-start | bytes 196612
  17.8 33.5 %copy-start.1 = (bf16[256,256]{1,0:T(8,128)(2,1)S(1)}, bf16[256,256]{1,0:T(8,128)(2,1)}, u32[]{:S(2)}) copy-start(bf16[256,256]{1,0:T(8,128)(2,1)} %constant.11.clone.turn) | copy-start | bytes 393220

commit v6 on v5

--- a/solution.py
+++ b/solution.py
@@ -103,6 +103,7 @@
     live_hbm,
     near_ref,
     basis_ref,
+    canvas_ref,
     coeff_ref,
     reflect_ref,
     row_ref,
@@ -156,6 +157,7 @@
         )
         copy.start()
         copies.append(copy)
+    canvas_ref[...] = jnp.zeros_like(canvas_ref)
     for copy in copies:
         copy.wait()
     basis_copy.wait()
@@ -169,9 +171,10 @@
         out_shape=[
             jax.ShapeDtypeStruct((3, 2, SLOTS + 8, 128), F32),
             jax.ShapeDtypeStruct((MODES, (LAST - FIRST) * TILE), BF16),
+            jax.ShapeDtypeStruct((2 * BLOCKS, WIDE, 128), F32),
         ],
         in_specs=[pl.BlockSpec(memory_space=pltpu.HBM)] * 6,
-        out_specs=[vmem, vmem],
+        out_specs=[vmem, vmem, vmem],
         scratch_shapes=[
             pltpu.VMEM((SLOTS, MODES), BF16),
             pltpu.VMEM((1, SLOTS), BF16),
@@ -213,7 +216,7 @@
 
 
 def render_kernel(
-    near, basis, canvas, left, right, marks, slots, table, tasks, slots_sem, table_sem
+    near, basis, clear, canvas, left, right, marks, slots, table, tasks, slots_sem, table_sem
 ):
     sector = lax.axis_index("sector")
     slab = lax.axis_index("slab")
@@ -237,7 +240,6 @@
                 marks[at, 3 + part : 4 + part, :] = reaches.astype(jnp.int32)
     table_copy = pltpu.make_async_copy(marks, table, table_sem)
     table_copy.start()
-    canvas[...] = jnp.zeros_like(canvas)
     coeff = [
         jnp.concatenate([near[hop, side, :SLOTS, :MODES] for side in range(2)], axis=0).astype(BF16)
         for hop in range(3)
@@ -322,13 +324,14 @@
         deposit(*before)
 
 
-def render(near, mode_basis):
+def render(near, basis, clear):
     vmem = pl.BlockSpec(memory_space=pltpu.VMEM)
     return pl.pallas_call(
         render_kernel,
         out_shape=jax.ShapeDtypeStruct((2 * BLOCKS, WIDE, 128), F32),
-        in_specs=[vmem, vmem],
+        in_specs=[vmem, vmem, vmem],
         out_specs=vmem,
+        input_output_aliases={2: 0},
         scratch_shapes=[
             pltpu.VMEM(((TILE + 2 * PAD) * WIDE, 128), F32),
             pltpu.VMEM(((TILE + 2 * PAD) * WIDE, 128), F32),
@@ -341,7 +344,7 @@
         ],
         compiler_params=pltpu.CompilerParams(vmem_limit_bytes=40 << 20),
         name="render_rows",
-    )(near, mode_basis)
+    )(near, basis, clear)
 
 
 def encode(value):
@@ -460,20 +463,20 @@
             inbox[0, :, sector] = early[:, sector]
             swap(0).wait()
 
-        @pl.loop(0, DEVICES // 16)
+        @pl.loop(0, DEVICES // 16, unroll=4)
         def _(step):
             codes_in = inbox[chunk, pl.ds(step * 8, 8)].astype(jnp.int32)
             plain[pl.ds(step * 16, 16), :CHUNK] = decode(codes_in).reshape(16, CHUNK, 128)
 
-        @pl.loop(0, CHUNK // 4)
+        @pl.loop(0, CHUNK // 8)
         def _(step):
             parts = []
-            for e in range(4):
-                turned = values[pl.ds(4 * step + e, DEVICES, stride=SHORT), :].T
+            for e in range(8):
+                turned = values[pl.ds(8 * step + e, DEVICES, stride=SHORT), :].T
                 parts.append(jnp.concatenate([turned[:64], turned[64:]], axis=1))
             mid = dot_long(jnp.concatenate(parts, axis=0), long_turn)
-            for e in range(4):
-                line = chunk * CHUNK + 4 * step + e
+            for e in range(8):
+                line = chunk * CHUNK + 8 * step + e
                 cos = twist[0, pl.ds(line, 1), :]
                 sin = twist[1, pl.ds(line, 1), :]
                 real = mid[64 * e : 64 * e + 64, :128]
@@ -558,8 +561,10 @@
 
 def body(mode_basis, mode_coeff, reflect, tile_row, tile_col, slot_live):
     turn, twist, long_turn, last_turn = (jnp.asarray(table) for table in tables())
-    near, basis = gather_near(mode_basis, mode_coeff, reflect, tile_row, tile_col, slot_live)
-    field = render(near, basis)
+    near, basis, clear = gather_near(
+        mode_basis, mode_coeff, reflect, tile_row, tile_col, slot_live
+    )
+    field = render(near, basis, clear)
     mid = exchange(field, turn, twist, long_turn)
     return finish(mid, last_turn)
 

time: 54.3 us -> 53.8 us (level)
    pallas_call x1, Pallas kernels: 33.5 us -> 32.8 us  [exchange(): pl.pallas_call(exchange_kernel, out_shape=jax.ShapeDtypeStruct((2, LINES,...]
where the time goes in v6:
time: 53.8 us; the launch traced here: 53.7 us
  Pallas kernels  53.6 us (100%)
    pallas_call x1, Pallas kernels, exchange(): pl.pallas_call(exchange_kernel, out_shape=jax.ShapeDtypeStruct((2, LINES,...  32.8 us
    pallas_call x1, Pallas kernels, gather_near(): pl.pallas_call(gather_kernel, out_shape=[jax.ShapeDtypeStruct((3, 2, SLOT...  13.3 us
    pallas_call x1, Pallas kernels, render(): pl.pallas_call(render_kernel, out_shape=jax.ShapeDtypeStruct((2 * BLOCKS,...  4.6 us
    pallas_call x1, Pallas kernels, finish(): pl.pallas_call(finish_kernel, out_shape=jax.ShapeDtypeStruct((2, LINES, G...  2.85 us

profile of v6, /device:TPU:1, one launch (start us, length us, event | category | flops | bytes accessed | tf_op | source)
XLA Modules:
  0.0 53.7 jit_solution(1128548218983446782)
XLA Ops:
  0.0 13.3 %gather_near.1 = (f32[3,2,24,128]{3,2,1,0:T(8,128)S(1)}, bf16[64,57344]{1,0:T(8,128)(2,1)S(1)}, f32[128,72,128]{2,1,0:T(8,128)S(1)}) custom-call(bf16[64,65536]{1,0:T(8,128)(2,1)} %basis_hbm.1, bf16[16,64]{1,0:T(8,128)(2,1)} %coeff_hbm.1, bf16[1,16]{1,0:T(2,128)(2,1)} %bitcast.4, s32[1,16]{1,0:T(1,128)} %bitcast.5, s32[1,16]{1,0:T(1,128)} %bitcast.6, ...), custom_call_target="tpu_custom_call" | custom-call | tf_op jit(solution)/shard_map/gather_near/pallas_call | solution.py:169
  13.3 0.0 copy-start
  13.4 0.0 copy-start.2
  13.4 0.0 copy-start.3
  13.4 4.6 %render_rows.1.field = f32[128,72,128]{2,1,0:T(8,128)S(1)} custom-call(f32[3,2,24,128]{3,2,1,0:T(8,128)S(1)} %get-tuple-element.8.near, bf16[64,57344]{1,0:T(8,128)(2,1)S(1)} %get-tuple-element.9.basis, f32[128,72,128]{2,1,0:T(8,128)S(1)} %get-tuple-element.10.clear), custom_call_target="tpu_custom_call", output_to_operand_aliasing={{}: (2, {})} | custom-call | tf_op jit(solution)/shard_map/render_rows/pallas_call | solution.py:329
  18.0 0.0 copy-done
  18.0 0.0 copy-done.2
  18.0 0.0 copy-done.3
  18.0 0.0 copy-start.1
  18.0 32.8 %exchange.1.mid_ref = f32[2,64,72,128]{3,2,1,0:T(8,128)S(1)} custom-call(f32[128,72,128]{2,1,0:T(8,128)S(1)} %render_rows.1.field, bf16[256,256]{1,0:T(8,128)(2,1)S(1)} %copy-done.2, f32[2,64,128]{2,1,0:T(8,128)S(1)} %copy-done.3, bf16[2,256,256]{2,1,0:T(8,128)(2,1)S(1)} %copy-done), custom_call_target="tpu_custom_call" | custom-call | tf_op jit(solution)/shard_map/exchange/pallas_call | solution.py:494
  50.9 0.0 copy-done.1
  50.9 2.8 %finish.1 = f32[2,64,8192]{2,1,0:T(8,128)} custom-call(f32[2,64,72,128]{3,2,1,0:T(8,128)S(1)} %exchange.1.mid_ref, bf16[256,256]{1,0:T(8,128)(2,1)S(1)} %copy-done.1), custom_call_target="tpu_custom_call" | custom-call | tf_op jit(solution)/shard_map/finish/pallas_call | solution.py:547
Async XLA Ops:
  13.3 4.6 %copy-start = (bf16[2,256,256]{2,1,0:T(8,128)(2,1)S(1)}, bf16[2,256,256]{2,1,0:T(8,128)(2,1)}, u32[]{:S(2)}) copy-start(bf16[2,256,256]{2,1,0:T(8,128)(2,1)} %constant.10.clone.long_turn) | copy-start | bytes 786436
  13.4 4.6 %copy-start.2 = (bf16[256,256]{1,0:T(8,128)(2,1)S(1)}, bf16[256,256]{1,0:T(8,128)(2,1)}, u32[]{:S(2)}) copy-start(bf16[256,256]{1,0:T(8,128)(2,1)} %constant.8.clone.turn) | copy-start | bytes 393220
  13.4 4.6 %copy-start.3 = (f32[2,64,128]{2,1,0:T(8,128)S(1)}, f32[2,64,128]{2,1,0:T(8,128)}, u32[]{:S(2)}) copy-start(f32[2,64,128]{2,1,0:T(8,128)} %constant.9.clone.twist) | copy-start | bytes 196612
  18.0 32.9 %copy-start.1 = (bf16[256,256]{1,0:T(8,128)(2,1)S(1)}, bf16[256,256]{1,0:T(8,128)(2,1)}, u32[]{:S(2)}) copy-start(bf16[256,256]{1,0:T(8,128)(2,1)} %constant.11.clone.turn) | copy-start | bytes 393220

commit v7 on v6

--- a/solution.py
+++ b/solution.py
@@ -209,10 +209,10 @@
     return 1.0 - double * sine, double * cosine
 
 
-TOGETHER = 28
+TOGETHER = 56
 STEPS_EACH = (LAST - FIRST) // 2 // TOGETHER
 LISTED = NEAR // STEPS_EACH
-TASKS = 4
+TASKS = 8
 
 
 def render_kernel(
@@ -386,7 +386,7 @@
 
     greet((other_sector, slab))
 
-    @pl.loop(1, SLABS, unroll=9)
+    @pl.loop(1, SLABS, unroll=21)
     def _(step):
         greet((sector, (slab + step) & (SLABS - 1)))
 

time: 53.8 us -> 53.6 us (level)
  no operation moved by 1% of the time
where the time goes in v7:
time: 53.6 us; the launch traced here: 53.5 us
  Pallas kernels  53.4 us (100%)
    pallas_call x1, Pallas kernels, exchange(): pl.pallas_call(exchange_kernel, out_shape=jax.ShapeDtypeStruct((2, LINES,...  33 us
    pallas_call x1, Pallas kernels, gather_near(): pl.pallas_call(gather_kernel, out_shape=[jax.ShapeDtypeStruct((3, 2, SLOT...  13.3 us
    pallas_call x1, Pallas kernels, render(): pl.pallas_call(render_kernel, out_shape=jax.ShapeDtypeStruct((2 * BLOCKS,...  4.2 us
    pallas_call x1, Pallas kernels, finish(): pl.pallas_call(finish_kernel, out_shape=jax.ShapeDtypeStruct((2, LINES, G...  2.85 us

profile of v7, /device:TPU:1, one launch (start us, length us, event | category | flops | bytes accessed | tf_op | source)
XLA Modules:
  0.0 53.5 jit_solution(6124094004159835855)
XLA Ops:
  0.0 13.3 %gather_near.1 = (f32[3,2,24,128]{3,2,1,0:T(8,128)S(1)}, bf16[64,57344]{1,0:T(8,128)(2,1)S(1)}, f32[128,72,128]{2,1,0:T(8,128)S(1)}) custom-call(bf16[64,65536]{1,0:T(8,128)(2,1)} %basis_hbm.1, bf16[16,64]{1,0:T(8,128)(2,1)} %coeff_hbm.1, bf16[1,16]{1,0:T(2,128)(2,1)} %bitcast.4, s32[1,16]{1,0:T(1,128)} %bitcast.5, s32[1,16]{1,0:T(1,128)} %bitcast.6, ...), custom_call_target="tpu_custom_call" | custom-call | tf_op jit(solution)/shard_map/gather_near/pallas_call | solution.py:169
  13.3 0.0 copy-start
  13.4 0.0 copy-start.2
  13.4 0.0 copy-start.3
  13.4 4.2 %render_rows.1.field = f32[128,72,128]{2,1,0:T(8,128)S(1)} custom-call(f32[3,2,24,128]{3,2,1,0:T(8,128)S(1)} %get-tuple-element.8.near, bf16[64,57344]{1,0:T(8,128)(2,1)S(1)} %get-tuple-element.9.basis, f32[128,72,128]{2,1,0:T(8,128)S(1)} %get-tuple-element.10.clear), custom_call_target="tpu_custom_call", output_to_operand_aliasing={{}: (2, {})} | custom-call | tf_op jit(solution)/shard_map/render_rows/pallas_call | solution.py:329
  17.6 0.0 copy-done
  17.6 0.0 copy-done.2
  17.6 0.0 copy-done.3
  17.6 0.0 copy-start.1
  17.6 33.0 %exchange.1.mid_ref = f32[2,64,72,128]{3,2,1,0:T(8,128)S(1)} custom-call(f32[128,72,128]{2,1,0:T(8,128)S(1)} %render_rows.1.field, bf16[256,256]{1,0:T(8,128)(2,1)S(1)} %copy-done.2, f32[2,64,128]{2,1,0:T(8,128)S(1)} %copy-done.3, bf16[2,256,256]{2,1,0:T(8,128)(2,1)S(1)} %copy-done), custom_call_target="tpu_custom_call" | custom-call | tf_op jit(solution)/shard_map/exchange/pallas_call | solution.py:494
  50.7 0.0 copy-done.1
  50.7 2.8 %finish.1 = f32[2,64,8192]{2,1,0:T(8,128)} custom-call(f32[2,64,72,128]{3,2,1,0:T(8,128)S(1)} %exchange.1.mid_ref, bf16[256,256]{1,0:T(8,128)(2,1)S(1)} %copy-done.1), custom_call_target="tpu_custom_call" | custom-call | tf_op jit(solution)/shard_map/finish/pallas_call | solution.py:547
Async XLA Ops:
  13.3 4.2 %copy-start = (bf16[2,256,256]{2,1,0:T(8,128)(2,1)S(1)}, bf16[2,256,256]{2,1,0:T(8,128)(2,1)}, u32[]{:S(2)}) copy-start(bf16[2,256,256]{2,1,0:T(8,128)(2,1)} %constant.10.clone.long_turn) | copy-start | bytes 786436
  13.4 4.2 %copy-start.2 = (bf16[256,256]{1,0:T(8,128)(2,1)S(1)}, bf16[256,256]{1,0:T(8,128)(2,1)}, u32[]{:S(2)}) copy-start(bf16[256,256]{1,0:T(8,128)(2,1)} %constant.8.clone.turn) | copy-start | bytes 393220
  13.4 4.2 %copy-start.3 = (f32[2,64,128]{2,1,0:T(8,128)S(1)}, f32[2,64,128]{2,1,0:T(8,128)}, u32[]{:S(2)}) copy-start(f32[2,64,128]{2,1,0:T(8,128)} %constant.9.clone.twist) | copy-start | bytes 196612
  17.6 33.1 %copy-start.1 = (bf16[256,256]{1,0:T(8,128)(2,1)S(1)}, bf16[256,256]{1,0:T(8,128)(2,1)}, u32[]{:S(2)}) copy-start(bf16[256,256]{1,0:T(8,128)(2,1)} %constant.11.clone.turn) | copy-start | bytes 393220

commit v8 on v7

--- a/solution.py
+++ b/solution.py
@@ -468,15 +468,17 @@
             codes_in = inbox[chunk, pl.ds(step * 8, 8)].astype(jnp.int32)
             plain[pl.ds(step * 16, 16), :CHUNK] = decode(codes_in).reshape(16, CHUNK, 128)
 
-        @pl.loop(0, CHUNK // 8)
+        each = CHUNK if chunk == CHUNKS - 1 else 8
+
+        @pl.loop(0, CHUNK // each)
         def _(step):
             parts = []
-            for e in range(8):
-                turned = values[pl.ds(8 * step + e, DEVICES, stride=SHORT), :].T
+            for e in range(each):
+                turned = values[pl.ds(each * step + e, DEVICES, stride=SHORT), :].T
                 parts.append(jnp.concatenate([turned[:64], turned[64:]], axis=1))
             mid = dot_long(jnp.concatenate(parts, axis=0), long_turn)
-            for e in range(8):
-                line = chunk * CHUNK + 8 * step + e
+            for e in range(each):
+                line = chunk * CHUNK + each * step + e
                 cos = twist[0, pl.ds(line, 1), :]
                 sin = twist[1, pl.ds(line, 1), :]
                 real = mid[64 * e : 64 * e + 64, :128]

time: 53.6 us -> 53.1 us (level)
    pallas_call x1, Pallas kernels: 33 us -> 32.1 us  [exchange(): pl.pallas_call(exchange_kernel, out_shape=jax.ShapeDtypeStruct((2, LINES,...]
where the time goes in v8:
time: 53.1 us; the launch traced here: 53 us
  Pallas kernels  52.9 us (100%)
    pallas_call x1, Pallas kernels, exchange(): pl.pallas_call(exchange_kernel, out_shape=jax.ShapeDtypeStruct((2, LINES,...  32.1 us
    pallas_call x1, Pallas kernels, gather_near(): pl.pallas_call(gather_kernel, out_shape=[jax.ShapeDtypeStruct((3, 2, SLOT...  13.3 us
    pallas_call x1, Pallas kernels, render(): pl.pallas_call(render_kernel, out_shape=jax.ShapeDtypeStruct((2 * BLOCKS,...  4.61 us
    pallas_call x1, Pallas kernels, finish(): pl.pallas_call(finish_kernel, out_shape=jax.ShapeDtypeStruct((2, LINES, G...  2.85 us

profile of v8, /device:TPU:1, one launch (start us, length us, event | category | flops | bytes accessed | tf_op | source)
XLA Modules:
  0.0 53.0 jit_solution(17066326266351659521)
XLA Ops:
  0.0 13.3 %gather_near.1 = (f32[3,2,24,128]{3,2,1,0:T(8,128)S(1)}, bf16[64,57344]{1,0:T(8,128)(2,1)S(1)}, f32[128,72,128]{2,1,0:T(8,128)S(1)}) custom-call(bf16[64,65536]{1,0:T(8,128)(2,1)} %basis_hbm.1, bf16[16,64]{1,0:T(8,128)(2,1)} %coeff_hbm.1, bf16[1,16]{1,0:T(2,128)(2,1)} %bitcast.4, s32[1,16]{1,0:T(1,128)} %bitcast.5, s32[1,16]{1,0:T(1,128)} %bitcast.6, ...), custom_call_target="tpu_custom_call" | custom-call | tf_op jit(solution)/shard_map/gather_near/pallas_call | solution.py:169
  13.3 0.0 copy-start
  13.4 0.0 copy-start.2
  13.4 0.0 copy-start.3
  13.4 4.6 %render_rows.1.field = f32[128,72,128]{2,1,0:T(8,128)S(1)} custom-call(f32[3,2,24,128]{3,2,1,0:T(8,128)S(1)} %get-tuple-element.8.near, bf16[64,57344]{1,0:T(8,128)(2,1)S(1)} %get-tuple-element.9.basis, f32[128,72,128]{2,1,0:T(8,128)S(1)} %get-tuple-element.10.clear), custom_call_target="tpu_custom_call", output_to_operand_aliasing={{}: (2, {})} | custom-call | tf_op jit(solution)/shard_map/render_rows/pallas_call | solution.py:329
  18.0 0.0 copy-done
  18.0 0.0 copy-done.2
  18.0 0.0 copy-done.3
  18.0 0.0 copy-start.1
  18.0 32.1 %exchange.1.mid_ref = f32[2,64,72,128]{3,2,1,0:T(8,128)S(1)} custom-call(f32[128,72,128]{2,1,0:T(8,128)S(1)} %render_rows.1.field, bf16[256,256]{1,0:T(8,128)(2,1)S(1)} %copy-done.2, f32[2,64,128]{2,1,0:T(8,128)S(1)} %copy-done.3, bf16[2,256,256]{2,1,0:T(8,128)(2,1)S(1)} %copy-done), custom_call_target="tpu_custom_call" | custom-call | tf_op jit(solution)/shard_map/exchange/pallas_call | solution.py:496
  50.1 0.0 copy-done.1
  50.1 2.9 %finish.1 = f32[2,64,8192]{2,1,0:T(8,128)} custom-call(f32[2,64,72,128]{3,2,1,0:T(8,128)S(1)} %exchange.1.mid_ref, bf16[256,256]{1,0:T(8,128)(2,1)S(1)} %copy-done.1), custom_call_target="tpu_custom_call" | custom-call | tf_op jit(solution)/shard_map/finish/pallas_call | solution.py:549
Async XLA Ops:
  13.3 4.7 %copy-start = (bf16[2,256,256]{2,1,0:T(8,128)(2,1)S(1)}, bf16[2,256,256]{2,1,0:T(8,128)(2,1)}, u32[]{:S(2)}) copy-start(bf16[2,256,256]{2,1,0:T(8,128)(2,1)} %constant.10.clone.long_turn) | copy-start | bytes 786436
  13.4 4.7 %copy-start.2 = (bf16[256,256]{1,0:T(8,128)(2,1)S(1)}, bf16[256,256]{1,0:T(8,128)(2,1)}, u32[]{:S(2)}) copy-start(bf16[256,256]{1,0:T(8,128)(2,1)} %constant.8.clone.turn) | copy-start | bytes 393220
  13.4 4.7 %copy-start.3 = (f32[2,64,128]{2,1,0:T(8,128)S(1)}, f32[2,64,128]{2,1,0:T(8,128)}, u32[]{:S(2)}) copy-start(f32[2,64,128]{2,1,0:T(8,128)} %constant.9.clone.twist) | copy-start | bytes 196612
  18.0 32.1 %copy-start.1 = (bf16[256,256]{1,0:T(8,128)(2,1)S(1)}, bf16[256,256]{1,0:T(8,128)(2,1)}, u32[]{:S(2)}) copy-start(bf16[256,256]{1,0:T(8,128)(2,1)} %constant.11.clone.turn) | copy-start | bytes 393220

commit v9 on v8

--- a/solution.py
+++ b/solution.py
@@ -386,7 +386,7 @@
 
     greet((other_sector, slab))
 
-    @pl.loop(1, SLABS, unroll=21)
+    @pl.loop(1, SLABS, unroll=63)
     def _(step):
         greet((sector, (slab + step) & (SLABS - 1)))
 
@@ -463,7 +463,7 @@
             inbox[0, :, sector] = early[:, sector]
             swap(0).wait()
 
-        @pl.loop(0, DEVICES // 16, unroll=4)
+        @pl.loop(0, DEVICES // 16, unroll=8 if chunk == CHUNKS - 1 else 4)
         def _(step):
             codes_in = inbox[chunk, pl.ds(step * 8, 8)].astype(jnp.int32)
             plain[pl.ds(step * 16, 16), :CHUNK] = decode(codes_in).reshape(16, CHUNK, 128)

time: 53.1 us -> 53.4 us (level)
    pallas_call x1, Pallas kernels: 4.61 us -> 3.79 us  [render(): pl.pallas_call(render_kernel, out_shape=jax.ShapeDtypeStruct((2 * BLOCKS,...]
    pallas_call x1, Pallas kernels: 32.1 us -> 32.8 us  [exchange(): pl.pallas_call(exchange_kernel, out_shape=jax.ShapeDtypeStruct((2, LINES,...]
where the time goes in v9:
time: 53.4 us; the launch traced here: 52.9 us
  Pallas kernels  52.8 us (99%)
    pallas_call x1, Pallas kernels, exchange(): pl.pallas_call(exchange_kernel, out_shape=jax.ShapeDtypeStruct((2, LINES,...  32.8 us
    pallas_call x1, Pallas kernels, gather_near(): pl.pallas_call(gather_kernel, out_shape=[jax.ShapeDtypeStruct((3, 2, SLOT...  13.3 us
    pallas_call x1, Pallas kernels, render(): pl.pallas_call(render_kernel, out_shape=jax.ShapeDtypeStruct((2 * BLOCKS,...  3.79 us
    pallas_call x1, Pallas kernels, finish(): pl.pallas_call(finish_kernel, out_shape=jax.ShapeDtypeStruct((2, LINES, G...  2.85 us

profile of v9, /device:TPU:1, one launch (start us, length us, event | category | flops | bytes accessed | tf_op | source)
XLA Modules:
  0.0 52.9 jit_solution(3804463521457657503)
XLA Ops:
  0.0 13.3 %gather_near.1 = (f32[3,2,24,128]{3,2,1,0:T(8,128)S(1)}, bf16[64,57344]{1,0:T(8,128)(2,1)S(1)}, f32[128,72,128]{2,1,0:T(8,128)S(1)}) custom-call(bf16[64,65536]{1,0:T(8,128)(2,1)} %basis_hbm.1, bf16[16,64]{1,0:T(8,128)(2,1)} %coeff_hbm.1, bf16[1,16]{1,0:T(2,128)(2,1)} %bitcast.4, s32[1,16]{1,0:T(1,128)} %bitcast.5, s32[1,16]{1,0:T(1,128)} %bitcast.6, ...), custom_call_target="tpu_custom_call" | custom-call | tf_op jit(solution)/shard_map/gather_near/pallas_call | solution.py:169
  13.3 0.0 copy-start
  13.4 0.0 copy-start.2
  13.4 0.0 copy-start.3
  13.4 3.8 %render_rows.1.field = f32[128,72,128]{2,1,0:T(8,128)S(1)} custom-call(f32[3,2,24,128]{3,2,1,0:T(8,128)S(1)} %get-tuple-element.8.near, bf16[64,57344]{1,0:T(8,128)(2,1)S(1)} %get-tuple-element.9.basis, f32[128,72,128]{2,1,0:T(8,128)S(1)} %get-tuple-element.10.clear), custom_call_target="tpu_custom_call", output_to_operand_aliasing={{}: (2, {})} | custom-call | tf_op jit(solution)/shard_map/render_rows/pallas_call | solution.py:329
  17.2 0.0 copy-done
  17.2 0.0 copy-done.2
  17.2 0.0 copy-done.3
  17.2 0.0 copy-start.1
  17.2 32.8 %exchange.1.mid_ref = f32[2,64,72,128]{3,2,1,0:T(8,128)S(1)} custom-call(f32[128,72,128]{2,1,0:T(8,128)S(1)} %render_rows.1.field, bf16[256,256]{1,0:T(8,128)(2,1)S(1)} %copy-done.2, f32[2,64,128]{2,1,0:T(8,128)S(1)} %copy-done.3, bf16[2,256,256]{2,1,0:T(8,128)(2,1)S(1)} %copy-done), custom_call_target="tpu_custom_call" | custom-call | tf_op jit(solution)/shard_map/exchange/pallas_call | solution.py:496
  50.0 0.0 copy-done.1
  50.0 2.9 %finish.1 = f32[2,64,8192]{2,1,0:T(8,128)} custom-call(f32[2,64,72,128]{3,2,1,0:T(8,128)S(1)} %exchange.1.mid_ref, bf16[256,256]{1,0:T(8,128)(2,1)S(1)} %copy-done.1), custom_call_target="tpu_custom_call" | custom-call | tf_op jit(solution)/shard_map/finish/pallas_call | solution.py:549
Async XLA Ops:
  13.3 3.8 %copy-start = (bf16[2,256,256]{2,1,0:T(8,128)(2,1)S(1)}, bf16[2,256,256]{2,1,0:T(8,128)(2,1)}, u32[]{:S(2)}) copy-start(bf16[2,256,256]{2,1,0:T(8,128)(2,1)} %constant.10.clone.long_turn) | copy-start | bytes 786436
  13.4 3.8 %copy-start.2 = (bf16[256,256]{1,0:T(8,128)(2,1)S(1)}, bf16[256,256]{1,0:T(8,128)(2,1)}, u32[]{:S(2)}) copy-start(bf16[256,256]{1,0:T(8,128)(2,1)} %constant.8.clone.turn) | copy-start | bytes 393220
  13.4 3.8 %copy-start.3 = (f32[2,64,128]{2,1,0:T(8,128)S(1)}, f32[2,64,128]{2,1,0:T(8,128)}, u32[]{:S(2)}) copy-start(f32[2,64,128]{2,1,0:T(8,128)} %constant.9.clone.twist) | copy-start | bytes 196612
  17.2 32.8 %copy-start.1 = (bf16[256,256]{1,0:T(8,128)(2,1)S(1)}, bf16[256,256]{1,0:T(8,128)(2,1)}, u32[]{:S(2)}) copy-start(bf16[256,256]{1,0:T(8,128)(2,1)} %constant.11.clone.turn) | copy-start | bytes 393220
